TPU v7x, 128 devices: a whole 4x4x4 slice. The times are simulated.
128 devices in a mesh: lat: 32 (over z, x, core), lon: 4 (over y).
Axes of the slice: x: 4, y: 4, z: 4, core: 2. Of those that a mesh axis runs over, the one named last changes fastest.
Arguments:
- grid_in: bfloat16 [131072, 227], P(('lat', 'lon')), may hold values from -6 to 6
- g2m_senders: int32 [98304], P(('lat', 'lon')), may hold values from 0 to 1023
- g2m_dest: int32 [98304, 1], P(('lat', 'lon')), may hold values from 0 to 8; in each aligned block of 768 rows (0 to 767, 768 to 1535, ...) at most 192 rows name the same one
- g2m_receivers: int32 [98304], P(('lat', 'lon')), may hold values from 0 to 319
- g2m_feat: bfloat16 [4, 98304], P(None, ('lat', 'lon')), may hold values from -6 to 6
- halo_near: int32 [128, 8, 64], P(('lat', 'lon')), may hold values from 0 to 319
- halo_far: int32 [128, 128, 2], P(('lat', 'lon')), may hold values from 0 to 319
- mesh_senders: int32 [327680], P(('lat', 'lon')), may hold values from 0 to 1087
- mesh_receivers: int32 [327680], P(('lat', 'lon')), may hold values from 0 to 319
- mesh_feat: bfloat16 [4, 327680], P(None, ('lat', 'lon')), may hold values from -6 to 6
- w_grid_in: bfloat16 [227, 512], replicated, may hold values from -0.375 to 0.375
- w_grid_out: bfloat16 [512, 512], replicated, may hold values from -0.25 to 0.25
- w_edge_latent: bfloat16 [512, 512], replicated, may hold values from -0.25 to 0.25
- w_edge_feat: bfloat16 [4, 512], replicated, may hold values from -3 to 3
- w_edge_out: bfloat16 [512, 512], replicated, may hold values from -0.25 to 0.25
- w_node_in: bfloat16 [512, 512], replicated, may hold values from -0.25 to 0.25
- w_node_out: bfloat16 [512, 512], replicated, may hold values from -0.25 to 0.25
- w_mesh_feat: bfloat16 [4, 512], replicated, may hold values from -3 to 3
- w_proc_edge: bfloat16 [512, 512], replicated, may hold values from -0.25 to 0.25
- w_proc_send: bfloat16 [512, 512], replicated, may hold values from -0.25 to 0.25
- w_proc_recv: bfloat16 [512, 512], replicated, may hold values from -0.25 to 0.25
- w_proc_out: bfloat16 [512, 512], replicated, may hold values from -0.25 to 0.25
- w_upd_self: bfloat16 [512, 512], replicated, may hold values from -0.25 to 0.25
- w_upd_sum: bfloat16 [512, 512], replicated, may hold values from -0.25 to 0.25
- w_upd_out: bfloat16 [512, 512], replicated, may hold values from -0.25 to 0.25
Outputs:
- mesh_out: bfloat16 [40960, 512], P(('lat', 'lon'))
- edge_out: bfloat16 [327680, 512], P(('lat', 'lon'))
Inputs may be any that keep to these rules, and one draw needn't show every extreme that they name: `g2m_dest`: at most 192 of one device's grid-to-mesh edges name the same code; in every draw some code is named by exactly 192 of some device's edges.
All inputs are finite; a program needn't handle non-finite values.
Results may differ from a plain program's by a relative error of at most 0.017.
Values may be sent and summed in bfloat16 or wider, within the bound.
A program may use at most 128 MiB of HBM per device.

v0:
```python
import jax
import jax.numpy as jnp
from jax import lax
from jax.sharding import PartitionSpec as P

MESH_DEV = 320


def with_halo(block, sides, width):
    for axis, dim in sides:
        count = lax.axis_size(axis)
        forward = [(i, i + 1) for i in range(count - 1)]
        forward.append((count - 1, 0))
        backward = [(target, source) for source, target in forward]
        low = lax.ppermute(
            lax.slice_in_dim(block, block.shape[dim] - width, None, axis=dim), axis, forward
        )
        high = lax.ppermute(lax.slice_in_dim(block, 0, width, axis=dim), axis, backward)
        block = jnp.concatenate([low, block, high], axis=dim)
    return block


def normalize(values):
    row_mean = jnp.mean(values, axis=-1, keepdims=True)
    centred = values - row_mean
    spread = jnp.mean(centred * centred, axis=-1, keepdims=True)
    return centred * lax.rsqrt(spread + 1e-05)


def product(left, right):
    return jnp.dot(left, right, preferred_element_type=jnp.float32)


def on_device(
    grid_in,
    g2m_senders,
    g2m_dest,
    g2m_receivers,
    g2m_feat,
    halo_near,
    halo_far,
    mesh_senders,
    mesh_receivers,
    mesh_feat,
    w_grid_in,
    w_grid_out,
    w_edge_latent,
    w_edge_feat,
    w_edge_out,
    w_node_in,
    w_node_out,
    w_mesh_feat,
    w_proc_edge,
    w_proc_send,
    w_proc_recv,
    w_proc_out,
    w_upd_self,
    w_upd_sum,
    w_upd_out,
):
    edge_count = g2m_senders.shape[0]
    latent_width = w_grid_out.shape[1]
    capacity = edge_count // 4
    grid_hidden = jax.nn.silu(product(grid_in, w_grid_in)).astype(jnp.bfloat16)
    grid_latent = normalize(product(grid_hidden, w_grid_out)).astype(jnp.bfloat16)
    codes = g2m_dest[:, 0]
    code_marks = (codes[:, None] == jnp.arange(9, dtype=jnp.int32)[None, :]).astype(jnp.int32)
    earlier = jnp.cumsum(code_marks, axis=0) - code_marks
    position = codes * capacity + jnp.sum(earlier * code_marks, axis=1)
    id_buffer = jnp.full((9 * capacity,), MESH_DEV, jnp.int32).at[position].set(g2m_receivers)
    id_padded = with_halo(id_buffer.reshape(3, 3, capacity), (("lat", 0), ("lon", 1)), 1)
    arrived_ids = id_padded[::2, ::2].reshape(-1)
    summed_in = product(grid_latent[g2m_senders], w_edge_latent) + product(g2m_feat.T, w_edge_feat)
    edge_hidden = jax.nn.silu(summed_in).astype(jnp.bfloat16)
    message = normalize(product(edge_hidden, w_edge_out)).astype(jnp.bfloat16)
    outgoing = (
        jnp.zeros((9 * capacity, latent_width), jnp.bfloat16)
        .at[position]
        .set(message)
        .reshape(3, 3, capacity, latent_width)
    )
    padded = with_halo(outgoing, (("lat", 0), ("lon", 1)), 1)
    arrived = padded[::2, ::2]
    messages = arrived.reshape(-1, latent_width)
    node_index = jnp.arange(MESH_DEV, dtype=jnp.int32)
    selector = (node_index[:, None] == arrived_ids[None, :]).astype(jnp.bfloat16)
    mesh_sum = product(selector, messages).astype(jnp.bfloat16)
    node_hidden = jax.nn.silu(product(mesh_sum, w_node_in)).astype(jnp.bfloat16)
    mesh_latent = normalize(product(node_hidden, w_node_out)).astype(jnp.bfloat16)
    near_rows = mesh_latent[halo_near[0]]
    blank = jnp.zeros((1,) + near_rows.shape[1:], jnp.bfloat16)
    near_block = jnp.concatenate([near_rows[:4], blank, near_rows[4:]], axis=0).reshape(
        3, 3, near_rows.shape[1], latent_width
    )
    near_padded = with_halo(near_block, (("lat", 0), ("lon", 1)), 1)
    near_in = near_padded[::2, ::2].reshape(9, -1, latent_width)
    near_arrived = jnp.concatenate([near_in[:4], near_in[5:]], axis=0).reshape(-1, latent_width)
    far_arrived = lax.all_to_all(
        mesh_latent[halo_far[0]], ("lat", "lon"), split_axis=0, concat_axis=0, tiled=True
    ).reshape(-1, latent_width)
    lookup = jnp.concatenate([mesh_latent, near_arrived, far_arrived], axis=0)
    edge_embed = product(mesh_feat.T, w_mesh_feat).astype(jnp.bfloat16)
    summed_edge = (
        product(edge_embed, w_proc_edge)
        + product(lookup[mesh_senders], w_proc_send)
        + product(mesh_latent[mesh_receivers], w_proc_recv)
    )
    proc_hidden = jax.nn.silu(summed_edge).astype(jnp.bfloat16)
    edge_out = (
        edge_embed.astype(jnp.float32) + normalize(product(proc_hidden, w_proc_out))
    ).astype(jnp.bfloat16)
    receive_mask = (node_index[:, None] == mesh_receivers[None, :]).astype(jnp.bfloat16)
    edge_sum = product(receive_mask, edge_out).astype(jnp.bfloat16)
    node_update = jax.nn.silu(
        product(mesh_latent, w_upd_self) + product(edge_sum, w_upd_sum)
    ).astype(jnp.bfloat16)
    mesh_out = (
        mesh_latent.astype(jnp.float32) + normalize(product(node_update, w_upd_out))
    ).astype(jnp.bfloat16)
    return (mesh_out, edge_out)


def solution(mesh):
    return jax.shard_map(
        on_device,
        mesh=mesh,
        in_specs=(
            P(("lat", "lon"), None),
            P(("lat", "lon")),
            P(("lat", "lon"), None),
            P(("lat", "lon")),
            P(None, ("lat", "lon")),
            P(("lat", "lon"), None, None),
            P(("lat", "lon"), None, None),
            P(("lat", "lon")),
            P(("lat", "lon")),
            P(None, ("lat", "lon")),
            P(),
            P(),
            P(),
            P(),
            P(),
            P(),
            P(),
            P(),
            P(),
            P(),
            P(),
            P(),
            P(),
            P(),
            P(),
        ),
        out_specs=(P(("lat", "lon"), None), P(("lat", "lon"), None)),
        check_vma=False,
    )
```

profile of v0, /device:TPU:1, one launch (start us, length us, event | category | flops | bytes accessed | tf_op | source)
XLA Modules:
  0.0 153.9 jit_solution(10534528721806618567)
XLA Ops:
  0.6 2.6 %fusion.30 = (f32[1024]{0:T(1024)S(1)}, f32[1024,512]{0,1:T(8,128)S(1)}) fusion(bf16[512,512]{1,0:T(8,128)(2,1)} %param.36, bf16[1024,227]{0,1:T(8,128)(2,1)} %param.25, bf16[227,512]{1,0:T(8,128)(2,1)} %param.35), kind=kOutput, calls=%fused_computation.96 | convolution fusion | flops 778042368 | bytes 3322880 | tf_op jit(solution)/shard_map/dot_general | solution.py:31
  3.2 0.3 multiply_reduce_fusion.1
  3.5 1.2 multiply_convert_fusion.1
  4.8 1.5 copy.30
  6.4 2.7 %gather_fusion = bf16[768,512]{1,0:T(8,128)(2,1)S(1)} fusion(bf16[1024,512]{1,0:T(8,128)(2,1)S(1)} %copy.30, s32[1024]{0:T(1024)S(1)} %pad_clamp_fusion.4), kind=kCustom, calls=%fused_computation | custom fusion | bytes 1575936 | tf_op jit(solution)/shard_map/gather | solution.py:73
  9.1 1.6 %fusion.35 = f32[768,512]{1,0:T(8,128)} fusion(bf16[4,768]{1,0:T(4,128)(2,1)S(1)} %copy-done.17, bf16[4,512]{1,0:T(4,128)(2,1)S(1)} %copy-done.18), kind=kOutput, calls=%fused_computation.101 | convolution fusion | flops 3145728 | bytes 1583104 | tf_op jit(solution)/shard_map/dot_general | solution.py:31
  10.6 2.6 %fusion.31 = (f32[768]{0:T(1024)S(1)}, f32[768,512]{0,1:T(8,128)S(1)}) fusion(bf16[512,512]{1,0:T(8,128)(2,1)S(1)} %copy-done.23, f32[768,512]{1,0:T(8,128)} %fusion.35, bf16[768,512]{1,0:T(8,128)(2,1)S(1)} %gather_fusion, bf16[512,512]{1,0:T(8,128)(2,1)} %param.37), kind=kOutput, calls=%fused_computation.97 | convolution fusion | flops 808058112 | bytes 4983808 | tf_op jit(solution)/shard_map/dot_general | solution.py:31
  13.6 1.2 copy.31
  14.8 1.7 %reduce-window.6 = s32[9,6,128]{2,0,1:T(8,128)S(1)} reduce-window(s32[9,6,128]{2,0,1:T(8,128)S(1)} %fusion.17, s32[]{:T(128)} %constant.20.clone.1), window={size=1x1x128 pad=0_0x0_0x127_0}, to_apply=%region_0.1 | reduce-window | flops 877824 | bytes 55300 | tf_op jit(solution)/shard_map/reduce-window
  16.5 0.3 slice_reduce_fusion
  17.1 6.6 %scatter_custom_fusion.1 = bf16[1728,512]{1,0:T(8,128)(2,1)S(1)} fusion(s32[768]{0:T(1024)S(1)} %fusion.20, bf16[768,512]{1,0:T(8,128)(2,1)} %copy.31, bf16[]{:T(256)} %constant.22.clone.1), kind=kCustom, calls=%fused_computation.37 | custom fusion | bytes 1769984 | tf_op jit(solution)/shard_map/scatter | solution.py:79
  23.7 1.1 fusion.24
  24.8 2.6 %collective-permute-start.4 = (bf16[1,3,192,512]{3,2,1,0:T(8,128)(2,1)}, bf16[1,3,192,512]{3,2,1,0:T(8,128)(2,1)S(1)}, u32[]{:S(2)}, u32[]{:S(2)}) collective-permute-start(bf16[1,3,192,512]{3,2,1,0:T(8,128)(2,1)} %bitcast.1), channel_id=1, source_target_pairs={{0,4},{4,8},{8,12},{12,16},{16,20},{20,24},{24,28},{28,32},{32,36}... | collective-permute-start | bytes 1769480 | tf_op jit(solution)/shard_map/ppermute | solution.py:15
  27.4 3.5 %scatter_custom_fusion = s32[1728]{0:T(1024)S(1)} fusion(s32[768]{0:T(1024)S(1)} %fusion.20, s32[768]{0:T(1024)} %param.28, s32[]{:T(128)} %constant.18.clone.1), kind=kCustom, calls=%fused_computation.77 | custom fusion | bytes 7424 | tf_op jit(solution)/shard_map/scatter | solution.py:70
  31.0 0.7 slice.104
  31.6 1.7 %collective-permute-start = (s32[1,3,192]{2,1,0:T(4,128)}, s32[1,3,192]{2,1,0:T(4,128)}, u32[]{:S(2)}, u32[]{:S(2)}) collective-permute-start(s32[1,3,192]{2,1,0:T(4,128)} %slice.104), channel_id=1, source_target_pairs={{0,4},{4,8},{8,12},{12,16},{16,20},{20,24},{24,28},{28,32},{32,36}... | collective-permute-start | bytes 6920 | tf_op jit(solution)/shard_map/ppermute | solution.py:15
  33.4 0.7 slice.106
  34.0 2.8 %collective-permute-start.1 = (s32[1,3,192]{2,1,0:T(4,128)}, s32[1,3,192]{2,1,0:T(4,128)}, u32[]{:S(2)}, u32[]{:S(2)}) collective-permute-start(s32[1,3,192]{2,1,0:T(4,128)} %slice.106), channel_id=1, source_target_pairs={{4,0},{8,4},{12,8},{16,12},{20,16},{24,20},{28,24},{32,28},{36,32}... | collective-permute-start | bytes 6920 | tf_op jit(solution)/shard_map/ppermute | solution.py:18
  36.9 0.6 compare_select_fusion
  37.5 0.9 convolution_convert_fusion
  38.4 3.9 %fusion.37 = f32[2560,512]{1,0:T(8,128)} fusion(bf16[2560,512]{1,0:T(8,128)(2,1)S(1)} %convolution_convert_fusion, bf16[512,512]{1,0:T(8,128)(2,1)S(1)} %copy-done.7), kind=kOutput, calls=%fused_computation.103 | convolution fusion | flops 1342177280 | bytes 8388608 | tf_op jit(solution)/shard_map/dot_general | solution.py:31
  42.3 1.5 %pad_maximum_fusion.5 = (bf16[5,1,192,512]{3,2,1,0:T(8,128)(2,1)}, bf16[5,1,192,512]{3,2,1,0:T(8,128)(2,1)}) fusion(bf16[1,3,192,512]{3,2,1,0:T(8,128)(2,1)S(1)} %collective-permute-done.5, bf16[3,3,192,512]{3,2,1,0:T(8,128)(2,1)S(1)} %bitcast.58, bf16[1,3,192,512]{3,2,1,0:T(8,128)(2,1)S(1)} %collective-permute-done.4), kind=kLoop, calls=%fused_computation.36 | loop fusion | flops 1966080 | bytes 4915200 | tf_op jit(solution)/shard_map/slice | solution.py:16
  43.9 1.3 collective-permute-start.6
  45.2 1.4 collective-permute-start.7
  46.6 0.5 compare_select_fusion.5
  47.1 0.7 reshape.183
  47.8 0.7 copy.32
  48.5 0.7 reshape.208
  49.3 0.7 constant_dynamic-update-slice_fusion.2
  50.0 0.7 constant_dynamic-update-slice_fusion.1
  50.7 0.7 constant_dynamic-update-slice_fusion
  51.5 2.6 %collective-permute-start.3 = (s32[5,1,192]{2,1,0:T(1,128)S(1)}, s32[5,1,192]{2,1,0:T(1,128)S(1)}, u32[]{:S(2)}, u32[]{:S(2)}) collective-permute-start(s32[5,1,192]{2,1,0:T(1,128)S(1)} %get-tuple-element.15), channel_id=1, source_target_pairs={{1,0},{2,1},{3,2},{0,3},{5,4},{6,5},{7,6},{4,7},{9,8},{10,9},{11,1... | collective-permute-start | bytes 11528 | tf_op jit(solution)/shard_map/ppermute | solution.py:18
  54.1 0.6 pad_clamp_fusion.2
  54.8 9.0 %collective-permute-done.2 = s32[5,1,192]{2,1,0:T(1,128)S(1)} collective-permute-done((s32[5,1,192]{2,1,0:T(1,128)S(1)}, s32[5,1,192]{2,1,0:T(1,128)S(1)}, u32[]{:S(2)}, u32[]{:S(2)}) %collective-permute-start.2) | collective-permute-done | bytes 3872 | tf_op jit(solution)/shard_map/ppermute | solution.py:15
  64.1 2.7 %pad_maximum_fusion = bf16[5,5,192,512]{3,2,1,0:T(8,128)(2,1)S(1)} fusion(bf16[5,1,192,512]{3,2,1,0:T(8,128)(2,1)} %collective-permute-done.7, bf16[1,3,192,512]{3,2,1,0:T(8,128)(2,1)S(1)} %collective-permute-done.5, bf16[3,3,192,512]{3,2,1,0:T(8,128)(2,1)S(1)} %bitcast.59, bf16[1,3,192,512]{3,2,1,0:T(8,128)(2,1)S(1)} %collective-permute-done.4, ...), kind=kLoop, calls=%fused_computation.10 | loop fusion | flops 9830400 | bytes 9830400 | tf_op jit(solution)/shard_map/concatenate | solution.py:19
  66.9 2.2 %multiply_convert_fusion.7 = bf16[320,512]{1,0:T(8,128)(2,1)S(1)} fusion(bf16[512,512]{1,0:T(8,128)(2,1)} %param.40, bf16[1728,512]{1,0:T(8,128)(2,1)S(1)} %bitcast.64, s32[1728]{0:T(1024)S(1)} %eq.62), kind=kOutput, calls=%fused_computation.45 | convolution fusion | flops 735539200 | bytes 2628352 | tf_op jit(solution)/shard_map/dot_general | solution.py:31
  69.1 0.4 fusion.32
  69.8 0.6 copy-done.4
  70.6 2.0 %gather_fusion.1 = bf16[512,512]{1,0:T(8,128)(2,1)S(1)} fusion(bf16[320,512]{1,0:T(8,128)(2,1)S(1)} %multiply_convert_fusion.6, s32[1024]{0:T(1024)S(1)} %get-tuple-element.29), kind=kCustom, calls=%fused_computation.1 | custom fusion | bytes 1050624 | tf_op jit(solution)/shard_map/gather | solution.py:90
  72.6 4.2 %collective-permute-start.8 = (bf16[1,3,64,512]{3,2,1,0:T(8,128)(2,1)S(1)}, bf16[1,3,64,512]{3,2,1,0:T(8,128)(2,1)S(1)}, u32[]{:S(2)}, u32[]{:S(2)}) collective-permute-start(bf16[1,3,64,512]{3,2,1,0:T(8,128)(2,1)S(1)} %bitcast.70), channel_id=1, source_target_pairs={{0,4},{4,8},{8,12},{12,16},{16,20},{20,24},{24,28},{28,32},{32,36}... | collective-permute-start | bytes 589832 | tf_op jit(solution)/shard_map/ppermute | solution.py:15
  76.9 1.8 %collective-permute-start.9 = (bf16[1,3,64,512]{3,2,1,0:T(8,128)(2,1)S(1)}, bf16[1,3,64,512]{3,2,1,0:T(8,128)(2,1)S(1)}, u32[]{:S(2)}, u32[]{:S(2)}) collective-permute-start(bf16[1,3,64,512]{3,2,1,0:T(8,128)(2,1)S(1)} %bitcast.69), channel_id=1, source_target_pairs={{4,0},{8,4},{12,8},{16,12},{20,16},{24,20},{28,24},{32,28},{36,32}... | collective-permute-start | bytes 589832 | tf_op jit(solution)/shard_map/ppermute | solution.py:18
  78.8 0.7 collective-permute-done.8
  79.6 2.4 %collective-permute-done.9 = bf16[1,3,64,512]{3,2,1,0:T(8,128)(2,1)S(1)} collective-permute-done((bf16[1,3,64,512]{3,2,1,0:T(8,128)(2,1)S(1)}, bf16[1,3,64,512]{3,2,1,0:T(8,128)(2,1)S(1)}, u32[]{:S(2)}, u32[]{:S(2)}) %collective-permute-start.9) | collective-permute-done | bytes 196640 | tf_op jit(solution)/shard_map/ppermute | solution.py:18
  82.0 0.9 pad_maximum_fusion.10
  82.9 1.3 collective-permute-start.10
  84.2 1.4 collective-permute-start.11
  85.6 1.2 gather_fusion.2
  86.7 0.8 reshape.207
  87.6 12.1 %all-to-all-start = ((bf16[128,2,512]{2,1,0:T(2,128)(2,1)}), bf16[128,2,512]{2,1,0:T(2,128)(2,1)S(1)}, u32[]{:S(2)}, u32[]{:S(2)}) async-start(bf16[128,2,512]{2,1,0:T(2,128)(2,1)} %reshape.207), calls=%async_computation | async-start | bytes 524288 | tf_op jit(solution)/shard_map/all_to_all | solution.py:98
  99.7 8.2 %gather_fusion.4 = bf16[2560,512]{1,0:T(8,128)(2,1)} fusion(bf16[320,512]{1,0:T(8,128)(2,1)S(1)} %multiply_convert_fusion.6, s32[3072]{0:T(1024)S(1)} %pad_clamp_fusion), kind=kCustom, calls=%fused_computation.4 | custom fusion | bytes 5253120 | tf_op jit(solution)/shard_map/gather | solution.py:106
  108.0 1.2 fusion.36
  109.2 1.7 %all-to-all-done = bf16[128,2,512]{2,1,0:T(2,128)(2,1)S(1)} async-done(((bf16[128,2,512]{2,1,0:T(2,128)(2,1)}), bf16[128,2,512]{2,1,0:T(2,128)(2,1)S(1)}, u32[]{:S(2)}, u32[]{:S(2)}) %all-to-all-start) | async-done | bytes 262176 | tf_op jit(solution)/shard_map/all_to_all | solution.py:98
  111.0 0.2 pad_maximum_fusion.1
  111.5 8.2 %gather_fusion.3 = bf16[2560,512]{1,0:T(8,128)(2,1)} fusion(bf16[1088,512]{1,0:T(8,128)(2,1)S(1)} %pad_maximum_fusion.2, s32[3072]{0:T(1024)S(1)} %pad_clamp_fusion.1), kind=kCustom, calls=%fused_computation.3 | custom fusion | bytes 5253120 | tf_op jit(solution)/shard_map/gather | solution.py:105
  119.7 5.8 %fusion.38 = f32[2560,512]{1,0:T(8,128)} fusion(bf16[2560,512]{1,0:T(8,128)(2,1)} %gather_fusion.3, bf16[512,512]{1,0:T(8,128)(2,1)} %param.44), kind=kOutput, calls=%fused_computation.104 | convolution fusion | flops 1342177280 | bytes 8388608 | tf_op jit(solution)/shard_map/dot_general | solution.py:31
  125.6 10.2 %fusion.33 = (f32[2560]{0:T(1024)S(1)}, f32[2560,512]{0,1:T(8,128)}) fusion(bf16[512,512]{1,0:T(8,128)(2,1)S(1)} %copy-done, f32[2560,512]{1,0:T(8,128)} %fusion.37, f32[2560,512]{1,0:T(8,128)} %fusion.38, bf16[2560,512]{1,0:T(8,128)(2,1)S(1)} %copy-done.6, bf16[512,512]{1,0:T(8,128)(2,1)} %param.45), kind=kOutput, calls=%fused_computation.99 | convolution fusion | flops 2694837760 | bytes 19408896 | tf_op jit(solution)/shard_map/dot_general | solution.py:31
  135.7 6.1 %copy.33 = f32[2560,512]{1,0:T(8,128)} copy(f32[2560,512]{0,1:T(8,128)} %get-tuple-element.25) | data formatting | bytes 10485760 | tf_op jit(solution)/shard_map/dot_general | solution.py:31
  141.8 3.5 %multiply_reduce_fusion = f32[2560]{0:T(1024)S(1)} fusion(f32[2560,512]{1,0:T(8,128)} %copy.33, f32[2560]{0:T(1024)S(1)} %broadcast_multiply_fusion), kind=kLoop, calls=%fused_computation.8 | loop fusion | flops 3929600 | bytes 5263360 | tf_op jit(solution)/shard_map/reduce_sum | solution.py:26
  145.3 0.5 copy-done.1
  145.8 2.5 %add_convert_fusion = bf16[2560,512]{1,0:T(8,128)(2,1)} fusion(bf16[2560,512]{1,0:T(8,128)(2,1)S(1)} %copy-done.3, f32[2560,512]{1,0:T(8,128)S(1)} %copy-done.1, f32[2560]{0:T(1024)S(1)} %add_rsqrt_fusion, f32[2560]{0:T(1024)S(1)} %broadcast_multiply_fusion), kind=kLoop, calls=%fused_computation.7 | loop fusion | flops 6553600 | bytes 10506240 | tf_op jit(solution)/shard_map/convert_element_type | solution.py:111
  148.4 3.4 %multiply_convert_fusion.5 = bf16[320,512]{1,0:T(8,128)(2,1)S(1)} fusion(f32[320,512]{1,0:T(8,128)} %fusion.36, bf16[512,512]{1,0:T(8,128)(2,1)} %param.48, bf16[2560,512]{1,0:T(8,128)(2,1)} %add_convert_fusion, s32[2560]{0:T(1024)S(1)} %copy-done.15), kind=kOutput, calls=%fused_computation.42 | convolution fusion | flops 1008599040 | bytes 4139008 | tf_op jit(solution)/shard_map/dot_general | solution.py:31
  151.8 0.4 fusion.34
  152.5 0.4 copy-done.5
  152.9 1.0 add_convert_fusion.1
  (102 shorter events, 2.6 us)
Async XLA Ops:
  0.6 124.9 %copy-start = (bf16[512,512]{1,0:T(8,128)(2,1)S(1)}, bf16[512,512]{1,0:T(8,128)(2,1)}, u32[]{:S(2)}) copy-start(bf16[512,512]{1,0:T(8,128)(2,1)} %param.46) | copy-start | bytes 1572868
  3.5 2.8 %copy-start.20 = (s32[768]{0:T(1024)S(1)}, s32[768]{0:T(1024)}, u32[]{:S(2)}) copy-start(s32[768]{0:T(1024)} %param.26) | copy-start | bytes 9220
  6.3 2.7 %copy-start.17 = (bf16[4,768]{1,0:T(4,128)(2,1)S(1)}, bf16[4,768]{1,0:T(4,128)(2,1)}, u32[]{:S(2)}) copy-start(bf16[4,768]{1,0:T(4,128)(2,1)} %param.29) | copy-start | bytes 18436
  6.3 2.7 %copy-start.18 = (bf16[4,512]{1,0:T(4,128)(2,1)S(1)}, bf16[4,512]{1,0:T(4,128)(2,1)}, u32[]{:S(2)}) copy-start(bf16[4,512]{1,0:T(4,128)(2,1)} %param.38) | copy-start | bytes 12292
  6.3 4.3 %copy-start.23 = (bf16[512,512]{1,0:T(8,128)(2,1)S(1)}, bf16[512,512]{1,0:T(8,128)(2,1)}, u32[]{:S(2)}) copy-start(bf16[512,512]{1,0:T(8,128)(2,1)} %param.39) | copy-start | bytes 1572868
  13.5 1.3 copy-start.16
  16.9 20.0 %copy-start.13 = (s32[2560]{0:T(1024)S(1)}, s32[2560]{0:T(1024)}, u32[]{:S(2)}) copy-start(s32[2560]{0:T(1024)} %param.32) | copy-start | bytes 30724
  16.9 19.9 %copy-start.14 = (s32[2560]{0:T(1024)S(1)}, s32[2560]{0:T(1024)}, u32[]{:S(2)}) copy-start(s32[2560]{0:T(1024)} %param.33) | copy-start | bytes 30724
  17.0 20.5 %copy-start.12 = (bf16[4,2560]{1,0:T(4,128)(2,1)S(1)}, bf16[4,2560]{1,0:T(4,128)(2,1)}, u32[]{:S(2)}) copy-start(bf16[4,2560]{1,0:T(4,128)(2,1)} %param.34) | copy-start | bytes 61444
  17.0 20.5 %copy-start.19 = (bf16[4,512]{1,0:T(4,128)(2,1)S(1)}, bf16[4,512]{1,0:T(4,128)(2,1)}, u32[]{:S(2)}) copy-start(bf16[4,512]{1,0:T(4,128)(2,1)} %param.42) | copy-start | bytes 12292
  23.7 14.7 %copy-start.21 = (s32[1,8,64]{2,1,0:T(8,128)S(1)}, s32[1,8,64]{2,1,0:T(8,128)}, u32[]{:S(2)}) copy-start(s32[1,8,64]{2,1,0:T(8,128)} %param.30) | copy-start | bytes 6148
  24.8 17.5 %collective-permute-start.4 = (bf16[1,3,192,512]{3,2,1,0:T(8,128)(2,1)}, bf16[1,3,192,512]{3,2,1,0:T(8,128)(2,1)S(1)}, u32[]{:S(2)}, u32[]{:S(2)}) collective-permute-start(bf16[1,3,192,512]{3,2,1,0:T(8,128)(2,1)} %bitcast.1), channel_id=1, source_target_pairs={{0,4},{4,8},{8,12},{12,16},{16,20},{20,24},{24,28},{28,32},{32,36}... | collective-permute-start | bytes 1769480 | tf_op jit(solution)/shard_map/ppermute | solution.py:15
  27.4 14.9 %collective-permute-start.5 = (bf16[1,3,192,512]{3,2,1,0:T(8,128)(2,1)}, bf16[1,3,192,512]{3,2,1,0:T(8,128)(2,1)S(1)}, u32[]{:S(2)}, u32[]{:S(2)}) collective-permute-start(bf16[1,3,192,512]{3,2,1,0:T(8,128)(2,1)} %bitcast.3), channel_id=1, source_target_pairs={{4,0},{8,4},{12,8},{16,12},{20,16},{24,20},{28,24},{32,28},{36,32}... | collective-permute-start | bytes 1769480 | tf_op jit(solution)/shard_map/ppermute | solution.py:18
  31.6 17.7 %collective-permute-start = (s32[1,3,192]{2,1,0:T(4,128)}, s32[1,3,192]{2,1,0:T(4,128)}, u32[]{:S(2)}, u32[]{:S(2)}) collective-permute-start(s32[1,3,192]{2,1,0:T(4,128)} %slice.104), channel_id=1, source_target_pairs={{0,4},{4,8},{8,12},{12,16},{16,20},{20,24},{24,28},{28,32},{32,36}... | collective-permute-start | bytes 6920 | tf_op jit(solution)/shard_map/ppermute | solution.py:15
  34.0 4.4 %copy-start.7 = (bf16[512,512]{1,0:T(8,128)(2,1)S(1)}, bf16[512,512]{1,0:T(8,128)(2,1)}, u32[]{:S(2)}) copy-start(bf16[512,512]{1,0:T(8,128)(2,1)} %param.43) | copy-start | bytes 1572868
  34.0 16.6 %collective-permute-start.1 = (s32[1,3,192]{2,1,0:T(4,128)}, s32[1,3,192]{2,1,0:T(4,128)}, u32[]{:S(2)}, u32[]{:S(2)}) collective-permute-start(s32[1,3,192]{2,1,0:T(4,128)} %slice.106), channel_id=1, source_target_pairs={{4,0},{8,4},{12,8},{16,12},{20,16},{24,20},{28,24},{32,28},{36,32}... | collective-permute-start | bytes 6920 | tf_op jit(solution)/shard_map/ppermute | solution.py:18
  38.4 3.9 %copy-start.2 = (bf16[2560,512]{1,0:T(8,128)(2,1)}, bf16[2560,512]{1,0:T(8,128)(2,1)S(1)}, u32[]{:S(2)}) copy-start(bf16[2560,512]{1,0:T(8,128)(2,1)S(1)} %convolution_convert_fusion) | copy-start | bytes 7864324
  42.3 4.3 %copy-start.22 = (s32[1,128,2]{1,2,0:T(2,128)S(1)}, s32[1,128,2]{1,2,0:T(2,128)}, u32[]{:S(2)}) copy-start(s32[1,128,2]{1,2,0:T(2,128)} %param.31) | copy-start | bytes 3076
  43.9 20.2 %collective-permute-start.6 = (bf16[5,1,192,512]{3,2,1,0:T(8,128)(2,1)}, bf16[5,1,192,512]{3,2,1,0:T(8,128)(2,1)}, u32[]{:S(2)}, u32[]{:S(2)}) collective-permute-start(bf16[5,1,192,512]{3,2,1,0:T(8,128)(2,1)} %get-tuple-element.2), channel_id=1, source_target_pairs={{0,1},{1,2},{2,3},{3,0},{4,5},{5,6},{6,7},{7,4},{8,9},{9,10},{10,1... | collective-permute-start | bytes 2949128 | tf_op jit(solution)/shard_map/ppermute | solution.py:15
  45.2 18.9 %collective-permute-start.7 = (bf16[5,1,192,512]{3,2,1,0:T(8,128)(2,1)}, bf16[5,1,192,512]{3,2,1,0:T(8,128)(2,1)}, u32[]{:S(2)}, u32[]{:S(2)}) collective-permute-start(bf16[5,1,192,512]{3,2,1,0:T(8,128)(2,1)} %get-tuple-element.3), channel_id=1, source_target_pairs={{1,0},{2,1},{3,2},{0,3},{5,4},{6,5},{7,6},{4,7},{9,8},{10,9},{11,1... | collective-permute-start | bytes 2949128 | tf_op jit(solution)/shard_map/ppermute | solution.py:18
  51.4 12.4 %collective-permute-start.2 = (s32[5,1,192]{2,1,0:T(1,128)S(1)}, s32[5,1,192]{2,1,0:T(1,128)S(1)}, u32[]{:S(2)}, u32[]{:S(2)}) collective-permute-start(s32[5,1,192]{2,1,0:T(1,128)S(1)} %get-tuple-element.14), channel_id=1, source_target_pairs={{0,1},{1,2},{2,3},{3,0},{4,5},{5,6},{6,7},{7,4},{8,9},{9,10},{10,1... | collective-permute-start | bytes 11528 | tf_op jit(solution)/shard_map/ppermute | solution.py:15
  51.5 12.3 %collective-permute-start.3 = (s32[5,1,192]{2,1,0:T(1,128)S(1)}, s32[5,1,192]{2,1,0:T(1,128)S(1)}, u32[]{:S(2)}, u32[]{:S(2)}) collective-permute-start(s32[5,1,192]{2,1,0:T(1,128)S(1)} %get-tuple-element.15), channel_id=1, source_target_pairs={{1,0},{2,1},{3,2},{0,3},{5,4},{6,5},{7,6},{4,7},{9,8},{10,9},{11,1... | collective-permute-start | bytes 11528 | tf_op jit(solution)/shard_map/ppermute | solution.py:18
  66.9 2.2 %copy-start.9 = (bf16[512,512]{1,0:T(8,128)(2,1)S(1)}, bf16[512,512]{1,0:T(8,128)(2,1)}, u32[]{:S(2)}) copy-start(bf16[512,512]{1,0:T(8,128)(2,1)} %param.41) | copy-start | bytes 1572868
  69.6 0.8 copy-start.4
  72.6 13.0 %copy-start.11 = (s32[2560]{0:T(1024)S(1)}, s32[2560]{0:T(1024)}, u32[]{:S(2)}) copy-start(s32[2560]{0:T(1024)} %compare_select_fusion) | copy-start | bytes 30724
  72.6 6.9 %collective-permute-start.8 = (bf16[1,3,64,512]{3,2,1,0:T(8,128)(2,1)S(1)}, bf16[1,3,64,512]{3,2,1,0:T(8,128)(2,1)S(1)}, u32[]{:S(2)}, u32[]{:S(2)}) collective-permute-start(bf16[1,3,64,512]{3,2,1,0:T(8,128)(2,1)S(1)} %bitcast.70), channel_id=1, source_target_pairs={{0,4},{4,8},{8,12},{12,16},{16,20},{20,24},{24,28},{28,32},{32,36}... | collective-permute-start | bytes 589832 | tf_op jit(solution)/shard_map/ppermute | solution.py:15
  76.9 5.1 %collective-permute-start.9 = (bf16[1,3,64,512]{3,2,1,0:T(8,128)(2,1)S(1)}, bf16[1,3,64,512]{3,2,1,0:T(8,128)(2,1)S(1)}, u32[]{:S(2)}, u32[]{:S(2)}) collective-permute-start(bf16[1,3,64,512]{3,2,1,0:T(8,128)(2,1)S(1)} %bitcast.69), channel_id=1, source_target_pairs={{4,0},{8,4},{12,8},{16,12},{20,16},{24,20},{28,24},{32,28},{36,32}... | collective-permute-start | bytes 589832 | tf_op jit(solution)/shard_map/ppermute | solution.py:18
  82.9 28.1 %collective-permute-start.10 = (bf16[5,1,64,512]{3,2,1,0:T(8,128)(2,1)}, bf16[5,1,64,512]{3,2,1,0:T(8,128)(2,1)S(1)}, u32[]{:S(2)}, u32[]{:S(2)}) collective-permute-start(bf16[5,1,64,512]{3,2,1,0:T(8,128)(2,1)} %get-tuple-element.6), channel_id=1, source_target_pairs={{0,1},{1,2},{2,3},{3,0},{4,5},{5,6},{6,7},{7,4},{8,9},{9,10},{10,1... | collective-permute-start | bytes 983048 | tf_op jit(solution)/shard_map/ppermute | solution.py:15
  84.2 26.8 %collective-permute-start.11 = (bf16[5,1,64,512]{3,2,1,0:T(8,128)(2,1)}, bf16[5,1,64,512]{3,2,1,0:T(8,128)(2,1)S(1)}, u32[]{:S(2)}, u32[]{:S(2)}) collective-permute-start(bf16[5,1,64,512]{3,2,1,0:T(8,128)(2,1)} %get-tuple-element.7), channel_id=1, source_target_pairs={{1,0},{2,1},{3,2},{0,3},{5,4},{6,5},{7,6},{4,7},{9,8},{10,9},{11,1... | collective-permute-start | bytes 983048 | tf_op jit(solution)/shard_map/ppermute | solution.py:18
  87.6 23.3 %all-to-all-start = ((bf16[128,2,512]{2,1,0:T(2,128)(2,1)}), bf16[128,2,512]{2,1,0:T(2,128)(2,1)S(1)}, u32[]{:S(2)}, u32[]{:S(2)}) async-start(bf16[128,2,512]{2,1,0:T(2,128)(2,1)} %reshape.207), calls=%async_computation | async-start | bytes 524288 | tf_op jit(solution)/shard_map/all_to_all | solution.py:98
  99.7 8.3 %copy-start.8 = (bf16[512,512]{1,0:T(8,128)(2,1)S(1)}, bf16[512,512]{1,0:T(8,128)(2,1)}, u32[]{:S(2)}) copy-start(bf16[512,512]{1,0:T(8,128)(2,1)} %param.47) | copy-start | bytes 1572868
  119.7 5.9 %copy-start.6 = (bf16[2560,512]{1,0:T(8,128)(2,1)S(1)}, bf16[2560,512]{1,0:T(8,128)(2,1)}, u32[]{:S(2)}) copy-start(bf16[2560,512]{1,0:T(8,128)(2,1)} %gather_fusion.4) | copy-start | bytes 7864324
  135.7 9.6 %copy-start.3 = (bf16[2560,512]{1,0:T(8,128)(2,1)S(1)}, bf16[2560,512]{1,0:T(8,128)(2,1)}, u32[]{:S(2)}) copy-start(bf16[2560,512]{1,0:T(8,128)(2,1)} %copy-done.2) | copy-start | bytes 7864324
  141.8 4.0 %copy-start.1 = (f32[2560,512]{1,0:T(8,128)S(1)}, f32[2560,512]{1,0:T(8,128)}, u32[]{:S(2)}) copy-start(f32[2560,512]{1,0:T(8,128)} %copy.33) | copy-start | bytes 15728644
  145.8 2.5 %copy-start.15 = (s32[2560]{0:T(1024)S(1)}, s32[2560]{0:T(1024)}, u32[]{:S(2)}) copy-start(s32[2560]{0:T(1024)} %param.33) | copy-start | bytes 30724
  148.4 3.4 %copy-start.10 = (bf16[512,512]{1,0:T(8,128)(2,1)S(1)}, bf16[512,512]{1,0:T(8,128)(2,1)}, u32[]{:S(2)}) copy-start(bf16[512,512]{1,0:T(8,128)(2,1)} %param.49) | copy-start | bytes 1572868
  151.8 1.1 copy-start.5
where the time goes:
time: 154 us
  local copies, waits for them, and re-layouts  51.2 us (33%)
  matrix products  35.2 us (23%)
  starting transfers between devices  33.5 us (22%)
  other arithmetic  18.9 us (12%)
  waiting for transfers between devices  13.8 us (9%)
    dot_general x12, matrix products, product(): return jnp.dot(left, right, preferred_element_type=jnp.float32)  35.2 us
    all_to_all x1, starting transfers between devices, on_device(): lax.all_to_all(mesh_latent[halo_far[0]], ('lat', 'lon'), split_axis=0, co...  12.1 us
    ppermute x6, starting transfers between devices, with_halo(): lax.ppermute(lax.slice_in_dim(block, block.shape[dim] - width, None, axis...  11.3 us
    ppermute x6, starting transfers between devices, with_halo(): lax.ppermute(lax.slice_in_dim(block, 0, width, axis=dim), axis, backward)  10.1 us
    ppermute x6, waiting for transfers between devices, with_halo(): lax.ppermute(lax.slice_in_dim(block, block.shape[dim] - width, None, axis...  9.74 us
    gather x1, local copies, waits for them, and re-layouts, on_device(): mesh_latent[mesh_receivers]  8.25 us
    gather x1, local copies, waits for them, and re-layouts, on_device(): lookup[mesh_senders]  8.23 us
    scatter x1, local copies, waits for them, and re-layouts, on_device(): outgoing = jnp.zeros((9 * capacity, latent_width), jnp.bfloat16).at[posit...  6.59 us
  transfers between devices with their start and end apart: 13, of which 4 were waited for; matrix products, arithmetic and copies ran while one was open for 19% of the time, Pallas kernels for 0%

commit v1 on v0

v1 whole, which is shorter than its diff:
```python
import functools

import jax
import jax.numpy as jnp
from jax import lax
from jax.experimental import pallas as pl
from jax.experimental.pallas import tpu as pltpu
from jax.sharding import PartitionSpec as P

F32 = jnp.float32
BF16 = jnp.bfloat16
I32 = jnp.int32
MESH = pl.DeviceIdType.MESH

N_LAT, N_LON = 32, 4
L = 512
CIN = 227
GRID_N = 1024
EDGES = 768
NODES = 320
MEDGES = 2560
CAP = 192
HCAP = 64
SLOT = CAP + 16
BLK = 256
NBLK = MEDGES // BLK

CODES = (1, 7, 3, 5, 0, 2, 6, 8)
SEND_ORDER = (4, 5, 6, 7, 2, 3, 0, 1)

COL_SEND = 0
COL_NEAR = 6
COL_FAR = 10
COL_MS = 12
COL_MR = 32

W_NAMES = (
    "wgo", "wel", "weo", "wni", "wno", "wpe", "wps", "wpr", "wpo", "wus", "wua", "wuo",
)


def dot(a, b):
    return jnp.dot(a, b, preferred_element_type=F32)


def dot_tn(a, b):
    return lax.dot_general(a, b, (((0,), (0,)), ((), ())), preferred_element_type=F32)


def dot_nt(a, b):
    return lax.dot_general(a, b, (((1,), (1,)), ((), ())), preferred_element_type=F32)


def silu(v):
    h = 0.5 * v
    return h + h * jnp.tanh(h)


def scaled(v):
    return v * lax.rsqrt(jnp.mean(v * v, axis=-1, keepdims=True) + 1e-05)


def normalize(v):
    c = v - jnp.mean(v, axis=-1, keepdims=True)
    return c * lax.rsqrt(jnp.mean(c * c, axis=-1, keepdims=True) + 1e-05)


def iota(shape, dim):
    return lax.broadcasted_iota(I32, shape, dim)


def hot(mask):
    return jnp.where(mask, 1.0, 0.0).astype(BF16)


def kernel(
    grid_hbm, idx_ref, dest_ref, recv_ref, gfeat_ref, mrow_ref, mfeat_ref, wgi_hbm, wef_ref, wmf_ref,
    wgo_h, wel_h, weo_h, wni_h, wno_h, wpe_h, wps_h, wpr_h, wpo_h, wus_h, wua_h, wuo_h,
    mesh_out, edge_out,
    graw, gsel, wraw, wpad32, wgi, wts, aux, wefp, featp, wcat,
    eout, ein, scol, rcol, apre, apost, rmask, gsend,
    tpre, tpost, near_out, a_out, a_in, b_out, pre, obuf, lat_buf, mbuf,
    in_sem, w_sem, es_sem, er_sem, ns_sem, nr_sem, as_sem, ar_sem, bs_sem, br_sem, o_sem,
):
    lat = lax.axis_index("lat")
    lon = lax.axis_index("lon")
    zx = lax.div(lat, 2)
    core = lax.rem(lat, 2)
    spot = core * 4 + lon

    def near_id(code):
        return (
            lax.rem(lat + (code // 3 - 1) + N_LAT, N_LAT),
            lax.rem(lon + (code % 3 - 1) + N_LON, N_LON),
        )

    def a_peer(i):
        other = lax.rem(zx + i, 16)
        return other, (other * 2 + core, lon)

    def b_peer(i):
        other = lax.rem(spot + i, 8)
        return other, (zx * 2 + lax.div(other, 4), lax.rem(other, 4))

    barrier = pltpu.get_barrier_semaphore()
    for code in CODES:
        pl.semaphore_signal(barrier, inc=1, device_id=near_id(code), device_id_type=MESH)

    def greet_a(i, carry):
        pl.semaphore_signal(barrier, inc=1, device_id=a_peer(i)[1], device_id_type=MESH)
        return carry

    def greet_b(i, carry):
        pl.semaphore_signal(barrier, inc=1, device_id=b_peer(i)[1], device_id_type=MESH)
        return carry

    lax.fori_loop(1, 16, greet_a, 0)
    lax.fori_loop(1, 8, greet_b, 0)

    g_copy = pltpu.make_async_copy(grid_hbm, graw, in_sem.at[0])
    g_copy.start()
    wi_copy = pltpu.make_async_copy(wgi_hbm, wraw, in_sem.at[1])
    wi_copy.start()
    w_copies = {}
    for k, (name, ref) in enumerate(
        zip(W_NAMES, (wgo_h, wel_h, weo_h, wni_h, wno_h, wpe_h, wps_h, wpr_h, wpo_h, wus_h, wua_h, wuo_h))
    ):
        w_copies[name] = pltpu.make_async_copy(ref, wts.at[k], w_sem.at[k])
        w_copies[name].start()

    def weight(name):
        return wts[W_NAMES.index(name)]

    codes = dest_ref[...]
    marks = jnp.where(iota((16, EDGES), 0) == codes, 1.0, 0.0)
    below = hot(iota((EDGES, EDGES), 0) < iota((EDGES, EDGES), 1))
    earlier = dot(marks.astype(BF16), below)
    rank = jnp.sum(earlier * marks, axis=0, keepdims=True).astype(I32)
    place = codes * CAP + rank

    name_row = recv_ref[...] + 1
    aux[...] = jnp.zeros_like(aux)
    aux[0:1, :] = lax.shift_right_logical(name_row, 4).astype(F32)
    aux[1:2, :] = lax.bitwise_and(name_row, 15).astype(F32)
    aux[4:8, :] = gfeat_ref[...].astype(F32)
    aux_rows = aux[...].astype(BF16)

    idx_t = jnp.transpose(idx_ref[...])

    g_copy.wait()
    gsel[:, 128:256] = jnp.zeros((EDGES, 128), BF16)
    for b in range(EDGES // 128):
        pick = hot(idx_t[:, COL_SEND + b : COL_SEND + b + 1] == iota((128, GRID_N), 1))
        gsel[b * 128 : (b + 1) * 128, 0:CIN] = dot(pick, graw[...]).astype(BF16)

    def pack(code, target, k):
        choose = hot(iota((CAP, EDGES), 0) + code * CAP == place)
        target[k, 0:CAP, :] = dot(choose, gsel[...]).astype(BF16)
        target[k, CAP:SLOT, :] = jnp.zeros((16, 256), BF16)
        target[k, CAP:SLOT, 0:CAP] = dot_nt(aux_rows, choose).astype(BF16)

    def edge_copy(k):
        return pltpu.make_async_remote_copy(
            src_ref=eout.at[k],
            dst_ref=ein.at[k],
            send_sem=es_sem.at[k],
            recv_sem=er_sem.at[k],
            device_id=near_id(CODES[k]),
            device_id_type=MESH,
        )

    for n, k in enumerate(SEND_ORDER):
        pack(CODES[k], eout, k)
        if n == 0:
            pl.semaphore_wait(barrier, 8 + 15 + 7)
        edge_copy(k).start()
    pack(4, ein, 8)

    wi_copy.wait()
    wpad32[224:256, :] = jnp.zeros((32, L), F32)
    wpad32[0:CIN, :] = wraw[...].astype(F32)
    wgi[...] = wpad32[...].astype(BF16)
    wefp[...] = jnp.zeros_like(wefp)
    wefp[4:8, :] = wef_ref[...].astype(F32)

    def centre(name):
        w_copies[name].wait()
        w = weight(name).astype(F32)
        wts[W_NAMES.index(name)] = (w - jnp.mean(w, axis=-1, keepdims=True)).astype(BF16)

    centre("wgo")
    w_copies["wel"].wait()
    centre("weo")

    def encode(slots, count):
        x = slots[:, 0:CAP, :].reshape(count * CAP, 256)
        h = silu(dot(x, wgi[...])).astype(BF16)
        latent = scaled(dot(h, weight("wgo"))).astype(BF16)
        wf = wefp[...].astype(BF16)
        tails = [slots[i, CAP:SLOT, :][:, 0:CAP] for i in range(count)]
        feat_part = jnp.concatenate([dot_tn(t, wf) for t in tails], axis=0) if count > 1 else dot_tn(tails[0], wf)
        h = silu(dot(latent, weight("wel")) + feat_part).astype(BF16)
        message = scaled(dot(h, weight("weo"))).astype(BF16)
        total = None
        for i in range(count):
            t = tails[i].astype(F32)
            node = (t[0:1, :] * 16.0 + t[1:2, :] - 1.0).astype(I32)
            part = dot(hot(iota((NODES, CAP), 0) == node), message[i * CAP : (i + 1) * CAP])
            total = part if total is None else total + part
        return total

    mbuf[...] = encode(ein[8:9], 1)

    for b in range(MEDGES // 128):
        scol[b] = jnp.broadcast_to(idx_t[:, COL_MS + b : COL_MS + b + 1], (128, 128))
        rcol[b] = jnp.broadcast_to(idx_t[:, COL_MR + b : COL_MR + b + 1], (128, 128))
    for b in range(6):
        gsend[b * 128 : (b + 1) * 128, :] = hot(idx_t[:, COL_NEAR + b : COL_NEAR + b + 1] == iota((128, NODES), 1))

    featp[...] = jnp.zeros_like(featp)
    featp[0:4, :] = mfeat_ref[...].astype(F32)

    def masks(b, carry):
        s = scol[b]
        r = rcol[b]
        lane = iota((128, 128), 1)
        rows = pl.ds(pl.multiple_of(b * 128, 128), 128)
        for t in range(5):
            if t < 2:
                m = s == lane + t * 128
            elif t == 2:
                m = ((s == lane + 256) & (lane < 64)) | (r == lane - 64)
            else:
                m = r == lane + (t * 128 - NODES)
            apre[rows, t * 128 : (t + 1) * 128] = hot(m)
        for t in range(4):
            apost[rows, t * 128 : (t + 1) * 128] = hot(s == lane + (NODES + t * 128))
        f = s - (NODES + 8 * HCAP)
        f = jnp.where(
            f >= 0,
            lax.shift_left(lax.bitwise_and(lax.shift_right_arithmetic(f, 1), 7), 5)
            + lax.shift_left(lax.shift_right_arithmetic(f, 4), 1)
            + lax.bitwise_and(f, 1),
            -1,
        )
        for t in range(2):
            apost[rows, 512 + t * 128 : 512 + (t + 1) * 128] = hot(f == lane + t * 128)
        lanes = pl.ds(pl.multiple_of(b * 128, 128), 128)
        rmask[:, lanes] = hot(iota((NODES, 128), 0) == mrow_ref[:, lanes])
        return carry

    lax.fori_loop(0, MEDGES // 128, masks, 0)

    centre("wpo")
    w_copies["wpe"].wait()
    wcat[...] = jnp.zeros_like(wcat)
    wcat[0:4, 0:L] = wmf_ref[...].astype(F32)
    wcat[:, L : 2 * L] = dot(wcat[:, 0:L].astype(BF16), weight("wpe"))

    def landed(k):
        return pltpu.make_async_remote_copy(
            src_ref=eout.at[k],
            dst_ref=ein.at[k],
            send_sem=es_sem.at[k],
            recv_sem=er_sem.at[k],
            device_id=near_id(CODES[0]),
            device_id_type=MESH,
        )

    def arrive(g, carry):
        for i in range(2):
            landed(2 * g + i).wait_recv()
        mbuf[...] += encode(ein[pl.ds(2 * g, 2)], 2)
        return carry

    lax.fori_loop(0, 4, arrive, 0)

    w_copies["wni"].wait()
    w_copies["wno"].wait()
    h = silu(dot(mbuf[...].astype(BF16), weight("wni"))).astype(BF16)
    latent = normalize(dot(h, weight("wno"))).astype(BF16)
    lat_buf[...] = latent
    w_copies["wps"].wait()
    own = dot(latent, weight("wps")).astype(BF16)
    tpre[0:NODES, :] = own
    near_out[...] = dot(gsend[0:512, :], own).astype(BF16).reshape(8, HCAP, L)

    def near_copy(e):
        return pltpu.make_async_remote_copy(
            src_ref=near_out.at[e],
            dst_ref=tpost.at[7 - e],
            send_sem=ns_sem.at[e],
            recv_sem=nr_sem.at[e],
            device_id=near_id(e if e < 4 else e + 1),
            device_id_type=MESH,
        )

    for e in (0, 2, 5, 7, 3, 4, 1, 6):
        near_copy(e).start()

    a_out[...] = dot(gsend[512:768, :], own).astype(BF16).reshape(16, 16, L)

    def a_copy(i):
        other, device = a_peer(i)
        return pltpu.make_async_remote_copy(
            src_ref=a_out.at[other],
            dst_ref=a_in.at[zx],
            send_sem=as_sem.at[i],
            recv_sem=ar_sem.at[i],
            device_id=device,
            device_id_type=MESH,
        )

    def a_start(i, carry):
        a_copy(i).start()
        return carry

    lax.fori_loop(1, 16, a_start, 0)
    a_in[zx] = a_out[zx]

    w_copies["wpr"].wait()
    tpre[NODES : 2 * NODES, :] = dot(latent, weight("wpr")).astype(BF16)

    def ahead(b, carry):
        rows = pl.ds(pl.multiple_of(b * BLK, BLK), BLK)
        embed = dot_tn(featp[:, rows].astype(BF16), wcat[...].astype(BF16))
        obuf[rows, :] = embed[:, 0:L].astype(BF16)
        pre[rows, :] = dot(apre[rows, :], tpre[...]) + embed[:, L : 2 * L]
        return carry

    lax.fori_loop(0, NBLK // 2, ahead, 0)

    def a_wait(i, carry):
        a_copy(i).wait_recv()
        return carry

    lax.fori_loop(1, 16, a_wait, 0)
    j = iota((256, 256), 0)
    source = (
        lax.shift_left(lax.bitwise_and(lax.shift_right_logical(j, 1), 15), 4)
        + lax.shift_left(lax.shift_right_logical(j, 5), 1)
        + lax.bitwise_and(j, 1)
    )
    turn = hot(iota((256, 256), 1) == source)
    b_out[...] = dot(turn, a_in[...].reshape(256, L)).astype(BF16).reshape(8, 32, L)

    def b_copy(i):
        other, device = b_peer(i)
        return pltpu.make_async_remote_copy(
            src_ref=b_out.at[other],
            dst_ref=tpost.at[8 + lax.div(spot, 2), pl.ds(pl.multiple_of(lax.rem(spot, 2) * 32, 32), 32)],
            send_sem=bs_sem.at[i],
            recv_sem=br_sem.at[i],
            device_id=device,
            device_id_type=MESH,
        )

    def b_start(i, carry):
        b_copy(i).start()
        return carry

    lax.fori_loop(1, 8, b_start, 0)
    tpost[8 + lax.div(spot, 2), pl.ds(pl.multiple_of(lax.rem(spot, 2) * 32, 32), 32), :] = b_out[spot]

    lax.fori_loop(NBLK // 2, NBLK, ahead, 0)

    for e in range(8):
        near_copy(e).wait_recv()

    def b_wait(i, carry):
        b_copy(i).wait_recv()
        return carry

    lax.fori_loop(1, 8, b_wait, 0)

    mbuf[...] = jnp.zeros_like(mbuf)

    def out_copy(b):
        rows = pl.ds(pl.multiple_of(b * BLK, BLK), BLK)
        return pltpu.make_async_copy(obuf.at[rows], edge_out.at[rows], o_sem.at[b])

    def process(b, carry):
        rows = pl.ds(pl.multiple_of(b * BLK, BLK), BLK)
        v = pre[rows, :] + dot(apost[rows, :], tpost[...].reshape(768, L))
        h = silu(v).astype(BF16)
        out = (obuf[rows, :].astype(F32) + scaled(dot(h, weight("wpo")))).astype(BF16)
        obuf[rows, :] = out
        out_copy(b).start()
        mbuf[...] += dot(rmask[:, rows], out)
        return carry

    lax.fori_loop(0, NBLK, process, 0)

    w_copies["wus"].wait()
    w_copies["wua"].wait()
    w_copies["wuo"].wait()
    h = dot(lat_buf[...], weight("wus")) + dot(mbuf[...].astype(BF16), weight("wua"))
    h = silu(h).astype(BF16)
    mesh_out[...] = (lat_buf[...].astype(F32) + normalize(dot(h, weight("wuo")))).astype(BF16)

    for k in range(8):
        edge_copy(k).wait_send()
        near_copy(k).wait_send()

    def a_sent(i, carry):
        a_copy(i).wait_send()
        return carry

    def b_sent(i, carry):
        b_copy(i).wait_send()
        return carry

    def o_sent(b, carry):
        out_copy(b).wait()
        return carry

    lax.fori_loop(1, 16, a_sent, 0)
    lax.fori_loop(1, 8, b_sent, 0)
    lax.fori_loop(0, NBLK, o_sent, 0)


def on_device(
    grid_in, g2m_senders, g2m_dest, g2m_receivers, g2m_feat, halo_near, halo_far, mesh_senders,
    mesh_receivers, mesh_feat, w_grid_in, w_grid_out, w_edge_latent, w_edge_feat, w_edge_out, w_node_in,
    w_node_out, w_mesh_feat, w_proc_edge, w_proc_send, w_proc_recv, w_proc_out, w_upd_self, w_upd_sum,
    w_upd_out,
):
    idx = jnp.concatenate(
        [
            g2m_senders, halo_near.reshape(-1), halo_far.reshape(-1), mesh_senders, mesh_receivers,
            jnp.zeros((128 * 128 - 52 * 128,), I32),
        ]
    ).reshape(128, 128)
    vm = pl.BlockSpec(memory_space=pltpu.VMEM)
    hb = pl.BlockSpec(memory_space=pl.ANY)
    dma = pltpu.SemaphoreType.DMA
    return pl.pallas_call(
        kernel,
        out_shape=(
            jax.ShapeDtypeStruct((NODES, L), BF16),
            jax.ShapeDtypeStruct((MEDGES, L), BF16),
        ),
        in_specs=[hb, vm, vm, vm, vm, vm, vm, hb, vm, vm] + [hb] * 12,
        out_specs=(vm, hb),
        scratch_shapes=[
            pltpu.VMEM((GRID_N, CIN), BF16),
            pltpu.VMEM((EDGES, 256), BF16),
            pltpu.VMEM((CIN, L), BF16),
            pltpu.VMEM((256, L), F32),
            pltpu.VMEM((256, L), BF16),
            pltpu.VMEM((12, L, L), BF16),
            pltpu.VMEM((16, EDGES), F32),
            pltpu.VMEM((16, L), F32),
            pltpu.VMEM((16, MEDGES), F32),
            pltpu.VMEM((16, 2 * L), F32),
            pltpu.VMEM((8, SLOT, 256), BF16),
            pltpu.VMEM((9, SLOT, 256), BF16),
            pltpu.VMEM((MEDGES // 128, 128, 128), I32),
            pltpu.VMEM((MEDGES // 128, 128, 128), I32),
            pltpu.VMEM((MEDGES, 2 * NODES), BF16),
            pltpu.VMEM((MEDGES, 768), BF16),
            pltpu.VMEM((NODES, MEDGES), BF16),
            pltpu.VMEM((768, NODES), BF16),
            pltpu.VMEM((2 * NODES, L), BF16),
            pltpu.VMEM((12, 64, L), BF16),
            pltpu.VMEM((8, HCAP, L), BF16),
            pltpu.VMEM((16, 16, L), BF16),
            pltpu.VMEM((16, 16, L), BF16),
            pltpu.VMEM((8, 32, L), BF16),
            pltpu.VMEM((MEDGES, L), F32),
            pltpu.VMEM((MEDGES, L), BF16),
            pltpu.VMEM((NODES, L), BF16),
            pltpu.VMEM((NODES, L), F32),
            dma((2,)),
            dma((12,)),
            dma((8,)),
            dma((8,)),
            dma((8,)),
            dma((8,)),
            dma((16,)),
            dma((16,)),
            dma((8,)),
            dma((8,)),
            dma((NBLK,)),
        ],
        compiler_params=pltpu.CompilerParams(
            collective_id=0, has_side_effects=True, vmem_limit_bytes=60 * 1024 * 1024
        ),
        cost_estimate=pl.CostEstimate(flops=15_000_000_000, bytes_accessed=12_000_000, transcendentals=4_000_000),
    )(
        grid_in, idx, g2m_dest.reshape(1, EDGES), g2m_receivers.reshape(1, EDGES), g2m_feat,
        mesh_receivers.reshape(1, MEDGES), mesh_feat, w_grid_in, w_edge_feat, w_mesh_feat,
        w_grid_out, w_edge_latent, w_edge_out, w_node_in, w_node_out, w_proc_edge, w_proc_send, w_proc_recv,
        w_proc_out, w_upd_self, w_upd_sum, w_upd_out,
    )


def solution(mesh):
    both = ("lat", "lon")
    rows, flat, cube = P(both, None), P(both), P(both, None, None)
    return jax.shard_map(
        on_device,
        mesh=mesh,
        in_specs=(rows, flat, rows, flat, P(None, both), cube, cube, flat, flat, P(None, both)) + (P(),) * 15,
        out_specs=(rows, rows),
        check_vma=False,
    )
```

time: 154 us -> 66.7 us (0.43)
  Pallas kernels: 0 us -> 52 us
  local copies, waits for them, and re-layouts: 51.2 us -> 13.6 us
  matrix products: 35.2 us -> 0 us
  starting transfers between devices: 33.5 us -> 0 us
  other arithmetic: 18.9 us -> 0.01 us
  waiting for transfers between devices: 13.8 us -> 0 us
    pallas_call x0 -> x1, Pallas kernels: none -> 52 us  [on_device(): pl.pallas_call(kernel, out_shape=(jax.ShapeDtypeStruct((NODES, L), BF16),...]
    dot_general x12 -> x0, matrix products: 35.2 us -> none  [product(): return jnp.dot(left, right, preferred_element_type=jnp.float32)]
    gather x6 -> x0, local copies, waits for them, and re-layouts: 23.1 us -> none  [the longest x1 8.25 us: on_device(): mesh_latent[mesh_receivers]]
    ppermute x12 -> x0, starting transfers between devices: 21.4 us -> none  [the longest x6 11.3 us: with_halo(): lax.ppermute(lax.slice_in_dim(block, block.shape[dim] - width, None, axis...]
    ppermute x12 -> x0, waiting for transfers between devices: 12.2 us -> none  [the longest x6 9.74 us: with_halo(): lax.ppermute(lax.slice_in_dim(block, block.shape[dim] - width, None, axis...]
    all_to_all x1 -> x0, starting transfers between devices: 12.1 us -> none  [on_device(): lax.all_to_all(mesh_latent[halo_far[0]], ('lat', 'lon'), split_axis=0, co...]
    scatter x2 -> x0, local copies, waits for them, and re-layouts: 10.1 us -> none  [the longest x1 6.59 us: on_device(): outgoing = jnp.zeros((9 * capacity, latent_width), jnp.bfloat16).at[posit...]
    unnamed x52 -> x11, local copies, waits for them, and re-layouts: 2.99 us -> 10.1 us
  transfers between devices with their start and end apart: 13 -> 0, of which waited for: 4 -> 0; matrix products, arithmetic and copies ran while one was open for 19% -> 0% of each run, Pallas kernels for 0% -> 0%
where the time goes in v1:
time: 66.7 us; the launch traced here: 66.2 us
  Pallas kernels  52 us (78%)
  local copies, waits for them, and re-layouts  13.6 us (20%)
    pallas_call x1, Pallas kernels, on_device(): pl.pallas_call(kernel, out_shape=(jax.ShapeDtypeStruct((NODES, L), BF16),...  52 us
    unnamed x11, local copies, waits for them, and re-layouts  10.1 us

profile of v1, /device:TPU:1, one launch (start us, length us, event | category | flops | bytes accessed | tf_op | source)
XLA Modules:
  0.0 66.2 jit_solution(16410345428992462513)
XLA Ops:
  0.6 0.8 %reshape.22 = s32[512]{0:T(512)S(1)} reshape(s32[1,8,64]{2,1,0:T(8,128)} %param.30) | data formatting | bytes 4096 | tf_op jit(solution)/shard_map/reshape | solution.py:430
  1.4 1.3 %reshape.26.recv_ref = s32[1,768]{1,0:T(1,128)} reshape(s32[768]{0:T(1024)} %param.28) | data formatting | bytes 6144 | tf_op jit(solution)/shard_map/reshape | solution.py:491
  2.7 1.3 %reshape.27.mrow_ref = s32[1,2560]{1,0:T(1,128)} reshape(s32[2560]{0:T(1024)} %param.33) | data formatting | bytes 20480 | tf_op jit(solution)/shard_map/reshape | solution.py:492
  4.0 0.8 %copy.28 = s32[1,128,2]{2,1,0:T(8,128)S(1)} copy(s32[1,128,2]{1,2,0:T(2,128)} %param.31) | data formatting | bytes 2048 | tf_op args[6]
  4.8 0.1 reshape.23
  4.9 0.7 %constant_dynamic-update-slice_fusion.4 = s32[16384]{0:T(1024)S(1)} fusion(s32[16384]{0:T(1024)S(1)} %custom-call, s32[768]{0:T(1024)} %param.26), kind=kLoop, calls=%fused_computation.5 | loop fusion | bytes 7168
  5.6 0.7 %constant_dynamic-update-slice_fusion.1 = s32[16384]{0:T(1024)S(1)} fusion(s32[16384]{0:T(1024)S(1)} %constant_dynamic-update-slice_fusion.2, s32[2560]{0:T(1024)} %param.32), kind=kLoop, calls=%fused_computation.2 | loop fusion | bytes 22528
  6.3 0.7 %constant_dynamic-update-slice_fusion = s32[16384]{0:T(1024)S(1)} fusion(s32[16384]{0:T(1024)S(1)} %constant_dynamic-update-slice_fusion.1, s32[2560]{0:T(1024)} %param.33), kind=kLoop, calls=%fused_computation.1 | loop fusion | bytes 22528
  7.1 0.0 copy-start
  7.1 2.0 %copy.29.grid_hbm = bf16[1024,227]{1,0:T(8,128)(2,1)} copy(bf16[1024,227]{0,1:T(8,128)(2,1)} %param.25) | data formatting | bytes 929792 | tf_op args[0]
  9.1 0.0 copy-done
  9.1 52.0 %shard_map.248 = (bf16[320,512]{1,0:T(8,128)(2,1)}, bf16[2560,512]{1,0:T(8,128)(2,1)}) custom-call(bf16[1024,227]{1,0:T(8,128)(2,1)} %copy.29.grid_hbm, s32[128,128]{1,0:T(8,128)} %bitcast.2, s32[1,768]{1,0:T(1,128)} %bitcast.3, s32[1,768]{1,0:T(1,128)} %reshape.26.recv_ref, bf16[4,768]{1,0:T(4,128)(2,1)} %gfeat_ref.1, s32[1,2560]{1,0:T(1,128)} %reshape.27.mrow_ref, ...), custom_call_target="tpu_custom_call" | custom-call | flops 15000000512 | bytes 12000000 | tf_op jit(solution)/shard_map/pallas_call | solution.py:437
  61.1 1.7 %copy.38 = bf16[320,512]{1,0:T(8,128)(2,1)} copy(bf16[320,512]{1,0:T(8,128)(2,1)} %get-tuple-element.4) | data formatting | bytes 655360
  62.8 3.4 %copy.39 = bf16[2560,512]{1,0:T(8,128)(2,1)} copy(bf16[2560,512]{1,0:T(8,128)(2,1)} %get-tuple-element.5) | data formatting | bytes 5242880
  (4 shorter events, 0.0 us)
Async XLA Ops:
  7.1 2.1 %copy-start = (s32[16384]{0:T(1024)}, s32[16384]{0:T(1024)S(1)}, u32[]{:S(2)}) copy-start(s32[16384]{0:T(1024)S(1)} %broadcast_dynamic-update-slice_fusion) | copy-start | bytes 196612

commit v2 on v1

--- a/solution.py
+++ b/solution.py
@@ -74,10 +74,11 @@
 
 
 def kernel(
-    grid_hbm, idx_ref, dest_ref, recv_ref, gfeat_ref, mrow_ref, mfeat_ref, wgi_hbm, wef_ref, wmf_ref,
+    grid_hbm, send_ref, dest_ref, recv_ref, gfeat_ref, near_ref, far_ref, msend_ref, mrecv_ref, mfeat_ref,
+    wgi_hbm, wef_ref, wmf_ref,
     wgo_h, wel_h, weo_h, wni_h, wno_h, wpe_h, wps_h, wpr_h, wpo_h, wus_h, wua_h, wuo_h,
     mesh_out, edge_out,
-    graw, gsel, wraw, wpad32, wgi, wts, aux, wefp, featp, wcat,
+    idx, mrow_ref, graw, gsel, wraw, wpad32, wgi, wts, aux, wefp, featp, wcat,
     eout, ein, scol, rcol, apre, apost, rmask, gsend,
     tpre, tpost, near_out, a_out, a_in, b_out, pre, obuf, lat_buf, mbuf,
     in_sem, w_sem, es_sem, er_sem, ns_sem, nr_sem, as_sem, ar_sem, bs_sem, br_sem, o_sem,
@@ -138,20 +139,28 @@
     rank = jnp.sum(earlier * marks, axis=0, keepdims=True).astype(I32)
     place = codes * CAP + rank
 
-    name_row = recv_ref[...] + 1
+    name_row = recv_ref[...].reshape(1, EDGES) + 1
     aux[...] = jnp.zeros_like(aux)
     aux[0:1, :] = lax.shift_right_logical(name_row, 4).astype(F32)
     aux[1:2, :] = lax.bitwise_and(name_row, 15).astype(F32)
     aux[4:8, :] = gfeat_ref[...].astype(F32)
     aux_rows = aux[...].astype(BF16)
 
-    idx_t = jnp.transpose(idx_ref[...])
+    idx[COL_SEND : COL_SEND + 6, :] = send_ref[...].reshape(6, 128)
+    for e in range(8):
+        idx[COL_NEAR + e // 2 : COL_NEAR + e // 2 + 1, e % 2 * 64 : e % 2 * 64 + 64] = near_ref[e : e + 1, :]
+    idx[COL_FAR : COL_FAR + 2, :] = far_ref[...]
+    idx[COL_MS : COL_MS + 20, :] = msend_ref[...].reshape(20, 128)
+    idx[COL_MR : COL_MR + 20, :] = mrecv_ref[...].reshape(20, 128)
+    idx[COL_MR + 20 :, :] = jnp.zeros((128 - COL_MR - 20, 128), I32)
+    mrow_ref[...] = mrecv_ref[...].reshape(1, MEDGES)
+    idx_t = jnp.transpose(idx[...])
 
     g_copy.wait()
     gsel[:, 128:256] = jnp.zeros((EDGES, 128), BF16)
     for b in range(EDGES // 128):
         pick = hot(idx_t[:, COL_SEND + b : COL_SEND + b + 1] == iota((128, GRID_N), 1))
-        gsel[b * 128 : (b + 1) * 128, 0:CIN] = dot(pick, graw[...]).astype(BF16)
+        gsel[b * 128 : (b + 1) * 128, 0:CIN] = dot_nt(pick, graw[...]).astype(BF16)
 
     def pack(code, target, k):
         choose = hot(iota((CAP, EDGES), 0) + code * CAP == place)
@@ -214,8 +223,20 @@
     for b in range(MEDGES // 128):
         scol[b] = jnp.broadcast_to(idx_t[:, COL_MS + b : COL_MS + b + 1], (128, 128))
         rcol[b] = jnp.broadcast_to(idx_t[:, COL_MR + b : COL_MR + b + 1], (128, 128))
-    for b in range(6):
-        gsend[b * 128 : (b + 1) * 128, :] = hot(idx_t[:, COL_NEAR + b : COL_NEAR + b + 1] == iota((128, NODES), 1))
+    def node_hot(c):
+        return hot(idx_t[:, c : c + 1] == iota((128, NODES), 1))
+
+    for b in range(4):
+        gsend[b * 128 : (b + 1) * 128, :] = node_hot(COL_NEAR + b)
+    j = iota((256, 256), 0)
+    source = (
+        lax.shift_left(lax.bitwise_and(lax.shift_right_logical(j, 3), 1), 7)
+        + lax.shift_left(lax.shift_right_logical(j, 4), 3)
+        + lax.bitwise_and(j, 7)
+    )
+    turn = hot(iota((256, 256), 1) == source)
+    far_hot = jnp.concatenate([node_hot(COL_FAR), node_hot(COL_FAR + 1)], axis=0)
+    gsend[512:768, :] = dot(turn, far_hot).astype(BF16)
 
     featp[...] = jnp.zeros_like(featp)
     featp[0:4, :] = mfeat_ref[...].astype(F32)
@@ -338,8 +359,8 @@
     j = iota((256, 256), 0)
     source = (
         lax.shift_left(lax.bitwise_and(lax.shift_right_logical(j, 1), 15), 4)
-        + lax.shift_left(lax.shift_right_logical(j, 5), 1)
-        + lax.bitwise_and(j, 1)
+        + lax.shift_left(lax.bitwise_and(j, 1), 3)
+        + lax.shift_right_logical(j, 5)
     )
     turn = hot(iota((256, 256), 1) == source)
     b_out[...] = dot(turn, a_in[...].reshape(256, L)).astype(BF16).reshape(8, 32, L)
@@ -425,12 +446,6 @@
     w_node_out, w_mesh_feat, w_proc_edge, w_proc_send, w_proc_recv, w_proc_out, w_upd_self, w_upd_sum,
     w_upd_out,
 ):
-    idx = jnp.concatenate(
-        [
-            g2m_senders, halo_near.reshape(-1), halo_far.reshape(-1), mesh_senders, mesh_receivers,
-            jnp.zeros((128 * 128 - 52 * 128,), I32),
-        ]
-    ).reshape(128, 128)
     vm = pl.BlockSpec(memory_space=pltpu.VMEM)
     hb = pl.BlockSpec(memory_space=pl.ANY)
     dma = pltpu.SemaphoreType.DMA
@@ -440,10 +455,12 @@
             jax.ShapeDtypeStruct((NODES, L), BF16),
             jax.ShapeDtypeStruct((MEDGES, L), BF16),
         ),
-        in_specs=[hb, vm, vm, vm, vm, vm, vm, hb, vm, vm] + [hb] * 12,
+        in_specs=[hb, vm, vm, vm, vm, vm, vm, vm, vm, vm, hb, vm, vm] + [hb] * 12,
         out_specs=(vm, hb),
         scratch_shapes=[
-            pltpu.VMEM((GRID_N, CIN), BF16),
+            pltpu.VMEM((128, 128), I32),
+            pltpu.VMEM((1, MEDGES), I32),
+            pltpu.VMEM((CIN, GRID_N), BF16),
             pltpu.VMEM((EDGES, 256), BF16),
             pltpu.VMEM((CIN, L), BF16),
             pltpu.VMEM((256, L), F32),
@@ -488,8 +505,8 @@
         ),
         cost_estimate=pl.CostEstimate(flops=15_000_000_000, bytes_accessed=12_000_000, transcendentals=4_000_000),
     )(
-        grid_in, idx, g2m_dest.reshape(1, EDGES), g2m_receivers.reshape(1, EDGES), g2m_feat,
-        mesh_receivers.reshape(1, MEDGES), mesh_feat, w_grid_in, w_edge_feat, w_mesh_feat,
+        grid_in.T, g2m_senders, g2m_dest.reshape(1, EDGES), g2m_receivers, g2m_feat,
+        halo_near.reshape(8, HCAP), halo_far.reshape(128, 2).T, mesh_senders, mesh_receivers, mesh_feat, w_grid_in, w_edge_feat, w_mesh_feat,
         w_grid_out, w_edge_latent, w_edge_out, w_node_in, w_node_out, w_proc_edge, w_proc_send, w_proc_recv,
         w_proc_out, w_upd_self, w_upd_sum, w_upd_out,
     )

time: 66.7 us -> 57.8 us (0.87)
  local copies, waits for them, and re-layouts: 13.6 us -> 5.12 us
    unnamed x11 -> x2, local copies, waits for them, and re-layouts: 10.1 us -> 5.12 us
    reshape x4 -> x0, local copies, waits for them, and re-layouts: 3.49 us -> none  [the longest x1 1.31 us: on_device(): mesh_receivers.reshape(1, MEDGES)]
where the time goes in v2:
time: 57.8 us; the launch traced here: 57.6 us
  Pallas kernels  51.8 us (90%)
  local copies, waits for them, and re-layouts  5.12 us (9%)
  between operations  0.65 us (1%)
    pallas_call x1, Pallas kernels, on_device(): pl.pallas_call(kernel, out_shape=(jax.ShapeDtypeStruct((NODES, L), BF16),...  51.8 us
    unnamed x2, local copies, waits for them, and re-layouts  5.12 us

profile of v2, /device:TPU:1, one launch (start us, length us, event | category | flops | bytes accessed | tf_op | source)
XLA Modules:
  0.0 57.6 jit_solution(567327226191817662)
XLA Ops:
  0.6 51.8 %shard_map.248 = (bf16[320,512]{1,0:T(8,128)(2,1)}, bf16[2560,512]{1,0:T(8,128)(2,1)}) custom-call(bf16[227,1024]{1,0:T(8,128)(2,1)} %bitcast.6, s32[768]{0:T(1024)} %send_ref.1, s32[1,768]{1,0:T(1,128)} %bitcast.8, s32[768]{0:T(1024)} %recv_ref.1, bf16[4,768]{1,0:T(4,128)(2,1)} %gfeat_ref.1, s32[8,64]{1,0:T(8,128)} %bitcast.7, s32[2,128]{1,0:T(2,128)} %bitcast.9, ...), custom_call_target="tpu_custom_call" | custom-call | flops 15000000512 | bytes 12000000 | tf_op jit(solution)/shard_map/pallas_call | solution.py:452
  52.5 1.7 %copy.29 = bf16[320,512]{1,0:T(8,128)(2,1)} copy(bf16[320,512]{1,0:T(8,128)(2,1)} %get-tuple-element.4) | data formatting | bytes 655360
  54.2 3.4 %copy.30 = bf16[2560,512]{1,0:T(8,128)(2,1)} copy(bf16[2560,512]{1,0:T(8,128)(2,1)} %get-tuple-element.5) | data formatting | bytes 5242880

commit v3 on v2

--- a/solution.py
+++ b/solution.py
@@ -24,6 +24,7 @@
 SLOT = CAP + 16
 BLK = 256
 NBLK = MEDGES // BLK
+AHEAD = 5
 
 CODES = (1, 7, 3, 5, 0, 2, 6, 8)
 SEND_ORDER = (4, 5, 6, 7, 2, 3, 0, 1)
@@ -63,6 +64,14 @@
 def normalize(v):
     c = v - jnp.mean(v, axis=-1, keepdims=True)
     return c * lax.rsqrt(jnp.mean(c * c, axis=-1, keepdims=True) + 1e-05)
+
+
+def far_order(kind):
+    j = iota((256, 256), 0)
+    row = lax.bitwise_and(j, 1)
+    if kind == 0:
+        return lax.bitwise_and(lax.shift_right_logical(j, 1), 7) * 32 + lax.shift_right_logical(j, 4) * 2 + row
+    return lax.bitwise_and(lax.shift_right_logical(j, 1), 15) * 16 + lax.shift_right_logical(j, 5) * 2 + row
 
 
 def iota(shape, dim):
@@ -80,8 +89,9 @@
     mesh_out, edge_out,
     idx, mrow_ref, graw, gsel, wraw, wpad32, wgi, wts, aux, wefp, featp, wcat,
     eout, ein, scol, rcol, apre, apost, rmask, gsend,
-    tpre, tpost, near_out, a_out, a_in, b_out, pre, obuf, lat_buf, mbuf,
-    in_sem, w_sem, es_sem, er_sem, ns_sem, nr_sem, as_sem, ar_sem, bs_sem, br_sem, o_sem,
+    tpre, tnear, tfar, near_out, a1_out, a1_in, b1_out, b1_in, b2_out, b2_in, a2_out, a2_in, hbuf,
+    pre, obuf, lat_buf, mbuf,
+    in_sem, w_sem, es_sem, er_sem, ns_sem, nr_sem, a1s, a1r, b1s, b1r, b2s, b2r, a2s, a2r, o_sem,
 ):
     lat = lax.axis_index("lat")
     lon = lax.axis_index("lon")
@@ -202,19 +212,17 @@
     centre("weo")
 
     def encode(slots, count):
-        x = slots[:, 0:CAP, :].reshape(count * CAP, 256)
-        h = silu(dot(x, wgi[...])).astype(BF16)
-        latent = scaled(dot(h, weight("wgo"))).astype(BF16)
         wf = wefp[...].astype(BF16)
         tails = [slots[i, CAP:SLOT, :][:, 0:CAP] for i in range(count)]
-        feat_part = jnp.concatenate([dot_tn(t, wf) for t in tails], axis=0) if count > 1 else dot_tn(tails[0], wf)
-        h = silu(dot(latent, weight("wel")) + feat_part).astype(BF16)
-        message = scaled(dot(h, weight("weo"))).astype(BF16)
+        v = [dot(slots[i, 0:CAP, :], wgi[...]) for i in range(count)]
+        v = [dot(silu(u).astype(BF16), weight("wgo")) for u in v]
+        v = [dot(scaled(u).astype(BF16), weight("wel")) + dot_tn(t, wf) for u, t in zip(v, tails)]
+        v = [dot(silu(u).astype(BF16), weight("weo")) for u in v]
         total = None
-        for i in range(count):
-            t = tails[i].astype(F32)
+        for u, t in zip(v, tails):
+            t = t.astype(F32)
             node = (t[0:1, :] * 16.0 + t[1:2, :] - 1.0).astype(I32)
-            part = dot(hot(iota((NODES, CAP), 0) == node), message[i * CAP : (i + 1) * CAP])
+            part = dot(hot(iota((NODES, CAP), 0) == node), scaled(u).astype(BF16))
             total = part if total is None else total + part
         return total
 
@@ -229,14 +237,13 @@
     for b in range(4):
         gsend[b * 128 : (b + 1) * 128, :] = node_hot(COL_NEAR + b)
     j = iota((256, 256), 0)
-    source = (
-        lax.shift_left(lax.bitwise_and(lax.shift_right_logical(j, 3), 1), 7)
-        + lax.shift_left(lax.shift_right_logical(j, 4), 3)
-        + lax.bitwise_and(j, 7)
-    )
-    turn = hot(iota((256, 256), 1) == source)
+    k = iota((256, 256), 1)
+    j_row = lax.bitwise_and(j, 1)
+    j_zx = lax.bitwise_and(lax.shift_right_logical(j, 1), 15)
+    j_spot = lax.shift_right_logical(j, 5)
     far_hot = jnp.concatenate([node_hot(COL_FAR), node_hot(COL_FAR + 1)], axis=0)
-    gsend[512:768, :] = dot(turn, far_hot).astype(BF16)
+    gsend[512:768, :] = dot(hot(k == j_row * 128 + lax.shift_right_logical(j, 1)), far_hot).astype(BF16)
+    gsend[768:1024, :] = dot(hot(k == j_row * 128 + j_zx * 8 + j_spot), far_hot).astype(BF16)
 
     featp[...] = jnp.zeros_like(featp)
     featp[0:4, :] = mfeat_ref[...].astype(F32)
@@ -257,13 +264,6 @@
         for t in range(4):
             apost[rows, t * 128 : (t + 1) * 128] = hot(s == lane + (NODES + t * 128))
         f = s - (NODES + 8 * HCAP)
-        f = jnp.where(
-            f >= 0,
-            lax.shift_left(lax.bitwise_and(lax.shift_right_arithmetic(f, 1), 7), 5)
-            + lax.shift_left(lax.shift_right_arithmetic(f, 4), 1)
-            + lax.bitwise_and(f, 1),
-            -1,
-        )
         for t in range(2):
             apost[rows, 512 + t * 128 : 512 + (t + 1) * 128] = hot(f == lane + t * 128)
         lanes = pl.ds(pl.multiple_of(b * 128, 128), 128)
@@ -304,40 +304,71 @@
     w_copies["wps"].wait()
     own = dot(latent, weight("wps")).astype(BF16)
     tpre[0:NODES, :] = own
-    near_out[...] = dot(gsend[0:512, :], own).astype(BF16).reshape(8, HCAP, L)
+
+    def a1_copy(i):
+        other, device = a_peer(i)
+        return pltpu.make_async_remote_copy(
+            src_ref=a1_out.at[other], dst_ref=a1_in.at[zx],
+            send_sem=a1s.at[i], recv_sem=a1r.at[i], device_id=device, device_id_type=MESH,
+        )
+
+    def b1_copy(i):
+        other, device = b_peer(i)
+        return pltpu.make_async_remote_copy(
+            src_ref=b1_out.at[other], dst_ref=b1_in.at[spot],
+            send_sem=b1s.at[i], recv_sem=b1r.at[i], device_id=device, device_id_type=MESH,
+        )
+
+    def a2_copy(i):
+        other, device = a_peer(i)
+        return pltpu.make_async_remote_copy(
+            src_ref=a2_out.at[other], dst_ref=a2_in.at[zx],
+            send_sem=a2s.at[i], recv_sem=a2r.at[i], device_id=device, device_id_type=MESH,
+        )
+
+    def b2_copy(i):
+        other, device = b_peer(i)
+        return pltpu.make_async_remote_copy(
+            src_ref=b2_out.at[other], dst_ref=b2_in.at[spot],
+            send_sem=b2s.at[i], recv_sem=b2r.at[i], device_id=device, device_id_type=MESH,
+        )
+
+    def each(count, make, act):
+        def step(i, carry):
+            act(make(i))
+            return carry
+
+        lax.fori_loop(1, count, step, 0)
+
+    def start(copy):
+        copy.start()
+
+    def arrived(copy):
+        copy.wait_recv()
+
+    def gone(copy):
+        copy.wait_send()
+
+    b1_out[...] = dot(gsend[768:1024, :], own[:, 256:512]).astype(BF16).reshape(8, 32, 256)
+    each(8, b1_copy, start)
+    a1_out[...] = dot(gsend[512:768, :], own[:, 0:256]).astype(BF16).reshape(16, 16, 256)
+    each(16, a1_copy, start)
 
     def near_copy(e):
         return pltpu.make_async_remote_copy(
             src_ref=near_out.at[e],
-            dst_ref=tpost.at[7 - e],
+            dst_ref=tnear.at[7 - e],
             send_sem=ns_sem.at[e],
             recv_sem=nr_sem.at[e],
             device_id=near_id(e if e < 4 else e + 1),
             device_id_type=MESH,
         )
 
+    near_out[...] = dot(gsend[0:512, :], own).astype(BF16).reshape(8, HCAP, L)
     for e in (0, 2, 5, 7, 3, 4, 1, 6):
         near_copy(e).start()
-
-    a_out[...] = dot(gsend[512:768, :], own).astype(BF16).reshape(16, 16, L)
-
-    def a_copy(i):
-        other, device = a_peer(i)
-        return pltpu.make_async_remote_copy(
-            src_ref=a_out.at[other],
-            dst_ref=a_in.at[zx],
-            send_sem=as_sem.at[i],
-            recv_sem=ar_sem.at[i],
-            device_id=device,
-            device_id_type=MESH,
-        )
-
-    def a_start(i, carry):
-        a_copy(i).start()
-        return carry
-
-    lax.fori_loop(1, 16, a_start, 0)
-    a_in[zx] = a_out[zx]
+    a1_in[zx] = a1_out[zx]
+    b1_in[spot] = b1_out[spot]
 
     w_copies["wpr"].wait()
     tpre[NODES : 2 * NODES, :] = dot(latent, weight("wpr")).astype(BF16)
@@ -349,50 +380,35 @@
         pre[rows, :] = dot(apre[rows, :], tpre[...]) + embed[:, L : 2 * L]
         return carry
 
-    lax.fori_loop(0, NBLK // 2, ahead, 0)
-
-    def a_wait(i, carry):
-        a_copy(i).wait_recv()
-        return carry
-
-    lax.fori_loop(1, 16, a_wait, 0)
-    j = iota((256, 256), 0)
-    source = (
-        lax.shift_left(lax.bitwise_and(lax.shift_right_logical(j, 1), 15), 4)
-        + lax.shift_left(lax.bitwise_and(j, 1), 3)
-        + lax.shift_right_logical(j, 5)
-    )
-    turn = hot(iota((256, 256), 1) == source)
-    b_out[...] = dot(turn, a_in[...].reshape(256, L)).astype(BF16).reshape(8, 32, L)
-
-    def b_copy(i):
-        other, device = b_peer(i)
-        return pltpu.make_async_remote_copy(
-            src_ref=b_out.at[other],
-            dst_ref=tpost.at[8 + lax.div(spot, 2), pl.ds(pl.multiple_of(lax.rem(spot, 2) * 32, 32), 32)],
-            send_sem=bs_sem.at[i],
-            recv_sem=br_sem.at[i],
-            device_id=device,
-            device_id_type=MESH,
-        )
-
-    def b_start(i, carry):
-        b_copy(i).start()
-        return carry
-
-    lax.fori_loop(1, 8, b_start, 0)
-    tpost[8 + lax.div(spot, 2), pl.ds(pl.multiple_of(lax.rem(spot, 2) * 32, 32), 32), :] = b_out[spot]
-
-    lax.fori_loop(NBLK // 2, NBLK, ahead, 0)
+    lax.fori_loop(0, AHEAD, ahead, 0)
+
+    each(8, b1_copy, arrived)
+    to_zx = hot(iota((256, 256), 1) == far_order(0))
+    a2_out[...] = dot(to_zx, b1_in[...].reshape(256, 256)).astype(BF16).reshape(16, 16, 256)
+    each(16, a2_copy, start)
+    each(16, a1_copy, arrived)
+    to_spot = hot(iota((256, 256), 1) == far_order(1))
+    b2_out[...] = dot(to_spot, a1_in[...].reshape(256, 256)).astype(BF16).reshape(8, 32, 256)
+    each(8, b2_copy, start)
+    a2_in[zx] = a2_out[zx]
+    b2_in[spot] = b2_out[spot]
+
+    lax.fori_loop(AHEAD, NBLK, ahead, 0)
 
     for e in range(8):
         near_copy(e).wait_recv()
 
-    def b_wait(i, carry):
-        b_copy(i).wait_recv()
-        return carry
-
-    lax.fori_loop(1, 8, b_wait, 0)
+    def near_part(b, carry):
+        rows = pl.ds(pl.multiple_of(b * BLK, BLK), BLK)
+        pre[rows, :] += dot(apost[rows, 0:512], tnear[...].reshape(512, L))
+        return carry
+
+    lax.fori_loop(0, NBLK, near_part, 0)
+
+    each(16, a2_copy, arrived)
+    each(8, b2_copy, arrived)
+    tfar[:, 0:256] = dot(to_zx, b2_in[...].reshape(256, 256)).astype(BF16)
+    tfar[:, 256:512] = a2_in[...].reshape(256, 256)
 
     mbuf[...] = jnp.zeros_like(mbuf)
 
@@ -400,22 +416,38 @@
         rows = pl.ds(pl.multiple_of(b * BLK, BLK), BLK)
         return pltpu.make_async_copy(obuf.at[rows], edge_out.at[rows], o_sem.at[b])
 
+    def hidden(b):
+        rows = pl.ds(pl.multiple_of(b * BLK, BLK), BLK)
+        return silu(pre[rows, :] + dot(apost[rows, 512:768], tfar[...])).astype(BF16)
+
+    def finish(b, h):
+        rows = pl.ds(pl.multiple_of(b * BLK, BLK), BLK)
+        return (obuf[rows, :].astype(F32) + scaled(dot(h, weight("wpo")))).astype(BF16)
+
+    hbuf[0] = hidden(0)
+
     def process(b, carry):
         rows = pl.ds(pl.multiple_of(b * BLK, BLK), BLK)
-        v = pre[rows, :] + dot(apost[rows, :], tpost[...].reshape(768, L))
-        h = silu(v).astype(BF16)
-        out = (obuf[rows, :].astype(F32) + scaled(dot(h, weight("wpo")))).astype(BF16)
+        out = finish(b, hbuf[lax.rem(b, 2)])
+        ahead_h = hidden(b + 1)
+        total = mbuf[...] + dot(rmask[:, rows], out)
         obuf[rows, :] = out
+        hbuf[lax.rem(b + 1, 2)] = ahead_h
+        mbuf[...] = total
         out_copy(b).start()
-        mbuf[...] += dot(rmask[:, rows], out)
-        return carry
-
-    lax.fori_loop(0, NBLK, process, 0)
+        return carry
+
+    lax.fori_loop(0, NBLK - 1, process, 0)
+    last = NBLK - 1
+    out = finish(last, hbuf[last % 2])
+    obuf[last * BLK : MEDGES, :] = out
+    out_copy(last).start()
+    edge_sum = (mbuf[...] + dot(rmask[:, last * BLK : MEDGES], out)).astype(BF16)
 
     w_copies["wus"].wait()
     w_copies["wua"].wait()
     w_copies["wuo"].wait()
-    h = dot(lat_buf[...], weight("wus")) + dot(mbuf[...].astype(BF16), weight("wua"))
+    h = dot(lat_buf[...], weight("wus")) + dot(edge_sum, weight("wua"))
     h = silu(h).astype(BF16)
     mesh_out[...] = (lat_buf[...].astype(F32) + normalize(dot(h, weight("wuo")))).astype(BF16)
 
@@ -423,20 +455,15 @@
         edge_copy(k).wait_send()
         near_copy(k).wait_send()
 
-    def a_sent(i, carry):
-        a_copy(i).wait_send()
-        return carry
-
-    def b_sent(i, carry):
-        b_copy(i).wait_send()
-        return carry
+    each(16, a1_copy, gone)
+    each(8, b1_copy, gone)
+    each(16, a2_copy, gone)
+    each(8, b2_copy, gone)
 
     def o_sent(b, carry):
         out_copy(b).wait()
         return carry
 
-    lax.fori_loop(1, 16, a_sent, 0)
-    lax.fori_loop(1, 8, b_sent, 0)
     lax.fori_loop(0, NBLK, o_sent, 0)
 
 
@@ -477,13 +504,20 @@
             pltpu.VMEM((MEDGES, 2 * NODES), BF16),
             pltpu.VMEM((MEDGES, 768), BF16),
             pltpu.VMEM((NODES, MEDGES), BF16),
-            pltpu.VMEM((768, NODES), BF16),
+            pltpu.VMEM((1024, NODES), BF16),
             pltpu.VMEM((2 * NODES, L), BF16),
-            pltpu.VMEM((12, 64, L), BF16),
             pltpu.VMEM((8, HCAP, L), BF16),
-            pltpu.VMEM((16, 16, L), BF16),
-            pltpu.VMEM((16, 16, L), BF16),
-            pltpu.VMEM((8, 32, L), BF16),
+            pltpu.VMEM((256, L), BF16),
+            pltpu.VMEM((8, HCAP, L), BF16),
+            pltpu.VMEM((16, 16, 256), BF16),
+            pltpu.VMEM((16, 16, 256), BF16),
+            pltpu.VMEM((8, 32, 256), BF16),
+            pltpu.VMEM((8, 32, 256), BF16),
+            pltpu.VMEM((8, 32, 256), BF16),
+            pltpu.VMEM((8, 32, 256), BF16),
+            pltpu.VMEM((16, 16, 256), BF16),
+            pltpu.VMEM((16, 16, 256), BF16),
+            pltpu.VMEM((2, BLK, L), BF16),
             pltpu.VMEM((MEDGES, L), F32),
             pltpu.VMEM((MEDGES, L), BF16),
             pltpu.VMEM((NODES, L), BF16),
@@ -498,6 +532,10 @@
             dma((16,)),
             dma((8,)),
             dma((8,)),
+            dma((8,)),
+            dma((8,)),
+            dma((16,)),
+            dma((16,)),
             dma((NBLK,)),
         ],
         compiler_params=pltpu.CompilerParams(

time: 57.8 us -> 54.9 us (0.950)
  Pallas kernels: 51.8 us -> 48.9 us
    pallas_call x1, Pallas kernels: 51.8 us -> 48.9 us  [on_device(): pl.pallas_call(kernel, out_shape=(jax.ShapeDtypeStruct((NODES, L), BF16),...]
where the time goes in v3:
time: 54.9 us; the launch traced here: 54.6 us
  Pallas kernels  48.9 us (89%)
  local copies, waits for them, and re-layouts  5.12 us (9%)
  between operations  0.65 us (1%)
    pallas_call x1, Pallas kernels, on_device(): pl.pallas_call(kernel, out_shape=(jax.ShapeDtypeStruct((NODES, L), BF16),...  48.9 us
    unnamed x2, local copies, waits for them, and re-layouts  5.12 us

profile of v3, /device:TPU:1, one launch (start us, length us, event | category | flops | bytes accessed | tf_op | source)
XLA Modules:
  0.0 54.6 jit_solution(9128729401396375488)
XLA Ops:
  0.6 48.9 %shard_map.248 = (bf16[320,512]{1,0:T(8,128)(2,1)}, bf16[2560,512]{1,0:T(8,128)(2,1)}) custom-call(bf16[227,1024]{1,0:T(8,128)(2,1)} %bitcast.6, s32[768]{0:T(1024)} %send_ref.1, s32[1,768]{1,0:T(1,128)} %bitcast.8, s32[768]{0:T(1024)} %recv_ref.1, bf16[4,768]{1,0:T(4,128)(2,1)} %gfeat_ref.1, s32[8,64]{1,0:T(8,128)} %bitcast.7, s32[2,128]{1,0:T(2,128)} %bitcast.9, ...), custom_call_target="tpu_custom_call" | custom-call | flops 15000000512 | bytes 12000000 | tf_op jit(solution)/shard_map/pallas_call | solution.py:479
  49.5 1.7 %copy.29 = bf16[320,512]{1,0:T(8,128)(2,1)} copy(bf16[320,512]{1,0:T(8,128)(2,1)} %get-tuple-element.4) | data formatting | bytes 655360
  51.2 3.4 %copy.30 = bf16[2560,512]{1,0:T(8,128)(2,1)} copy(bf16[2560,512]{1,0:T(8,128)(2,1)} %get-tuple-element.5) | data formatting | bytes 5242880

commit v4 on v3

--- a/solution.py
+++ b/solution.py
@@ -22,12 +22,12 @@
 CAP = 192
 HCAP = 64
 SLOT = CAP + 16
-BLK = 256
+TALL = 1280
+BLK = 640
 NBLK = MEDGES // BLK
-AHEAD = 5
 
 CODES = (1, 7, 3, 5, 0, 2, 6, 8)
-SEND_ORDER = (4, 5, 6, 7, 2, 3, 0, 1)
+SEND_ORDER = (2, 3, 0, 1, 4, 5, 6, 7)
 
 COL_SEND = 0
 COL_NEAR = 6
@@ -87,7 +87,7 @@
     wgi_hbm, wef_ref, wmf_ref,
     wgo_h, wel_h, weo_h, wni_h, wno_h, wpe_h, wps_h, wpr_h, wpo_h, wus_h, wua_h, wuo_h,
     mesh_out, edge_out,
-    idx, mrow_ref, graw, gsel, wraw, wpad32, wgi, wts, aux, wefp, featp, wcat,
+    idx, mrow_ref, graw, pick, gsel, wraw, wpad32, wgi, wts, aux, wefp, featp, wmf,
     eout, ein, scol, rcol, apre, apost, rmask, gsend,
     tpre, tnear, tfar, near_out, a1_out, a1_in, b1_out, b1_in, b2_out, b2_in, a2_out, a2_in, hbuf,
     pre, obuf, lat_buf, mbuf,
@@ -169,14 +169,20 @@
     g_copy.wait()
     gsel[:, 128:256] = jnp.zeros((EDGES, 128), BF16)
     for b in range(EDGES // 128):
-        pick = hot(idx_t[:, COL_SEND + b : COL_SEND + b + 1] == iota((128, GRID_N), 1))
-        gsel[b * 128 : (b + 1) * 128, 0:CIN] = dot_nt(pick, graw[...]).astype(BF16)
-
-    def pack(code, target, k):
-        choose = hot(iota((CAP, EDGES), 0) + code * CAP == place)
-        target[k, 0:CAP, :] = dot(choose, gsel[...]).astype(BF16)
-        target[k, CAP:SLOT, :] = jnp.zeros((16, 256), BF16)
-        target[k, CAP:SLOT, 0:CAP] = dot_nt(aux_rows, choose).astype(BF16)
+        pick[b * 128 : (b + 1) * 128, :] = hot(idx_t[:, COL_SEND + b : COL_SEND + b + 1] == iota((128, GRID_N), 1))
+    gsel[:, 0:CIN] = dot_nt(pick[...], graw[...]).astype(BF16)
+
+    def choice(code):
+        return hot(iota((CAP, EDGES), 0) + code * CAP == place)
+
+    def pack(jobs):
+        choose = jnp.concatenate([choice(code) for code, _, _ in jobs], axis=0)
+        rows = dot(choose, gsel[...]).astype(BF16)
+        tails = dot_nt(aux_rows, choose).astype(BF16)
+        for i, (_, target, k) in enumerate(jobs):
+            target[k, 0:CAP, :] = rows[i * CAP : (i + 1) * CAP]
+            target[k, CAP:SLOT, :] = jnp.zeros((16, 256), BF16)
+            target[k, CAP:SLOT, 0:CAP] = tails[:, i * CAP : (i + 1) * CAP]
 
     def edge_copy(k):
         return pltpu.make_async_remote_copy(
@@ -188,12 +194,13 @@
             device_id_type=MESH,
         )
 
-    for n, k in enumerate(SEND_ORDER):
-        pack(CODES[k], eout, k)
+    for n in range(0, 8, 4):
+        pack([(CODES[k], eout, k) for k in SEND_ORDER[n : n + 4]])
         if n == 0:
             pl.semaphore_wait(barrier, 8 + 15 + 7)
-        edge_copy(k).start()
-    pack(4, ein, 8)
+        for k in SEND_ORDER[n : n + 4]:
+            edge_copy(k).start()
+    pack([(4, ein, 8)])
 
     wi_copy.wait()
     wpad32[224:256, :] = jnp.zeros((32, L), F32)
@@ -214,15 +221,17 @@
     def encode(slots, count):
         wf = wefp[...].astype(BF16)
         tails = [slots[i, CAP:SLOT, :][:, 0:CAP] for i in range(count)]
-        v = [dot(slots[i, 0:CAP, :], wgi[...]) for i in range(count)]
-        v = [dot(silu(u).astype(BF16), weight("wgo")) for u in v]
-        v = [dot(scaled(u).astype(BF16), weight("wel")) + dot_tn(t, wf) for u, t in zip(v, tails)]
-        v = [dot(silu(u).astype(BF16), weight("weo")) for u in v]
+        v = dot(slots[:, 0:CAP, :].reshape(count * CAP, 256), wgi[...])
+        v = dot(silu(v).astype(BF16), weight("wgo"))
+        v = dot(scaled(v).astype(BF16), weight("wel"))
+        feat = [dot_tn(t, wf) for t in tails]
+        v = v + (jnp.concatenate(feat, axis=0) if count > 1 else feat[0])
+        message = scaled(dot(silu(v).astype(BF16), weight("weo"))).astype(BF16)
         total = None
-        for u, t in zip(v, tails):
+        for i, t in enumerate(tails):
             t = t.astype(F32)
             node = (t[0:1, :] * 16.0 + t[1:2, :] - 1.0).astype(I32)
-            part = dot(hot(iota((NODES, CAP), 0) == node), scaled(u).astype(BF16))
+            part = dot(hot(iota((NODES, CAP), 0) == node), message[i * CAP : (i + 1) * CAP])
             total = part if total is None else total + part
         return total
 
@@ -247,6 +256,7 @@
 
     featp[...] = jnp.zeros_like(featp)
     featp[0:4, :] = mfeat_ref[...].astype(F32)
+    apre[:, 640:768] = jnp.zeros((MEDGES, 128), BF16)
 
     def masks(b, carry):
         s = scol[b]
@@ -267,6 +277,7 @@
         for t in range(2):
             apost[rows, 512 + t * 128 : 512 + (t + 1) * 128] = hot(f == lane + t * 128)
         lanes = pl.ds(pl.multiple_of(b * 128, 128), 128)
+        apre[rows, 640:648] = jnp.transpose(featp[:, lanes]).astype(BF16)
         rmask[:, lanes] = hot(iota((NODES, 128), 0) == mrow_ref[:, lanes])
         return carry
 
@@ -274,9 +285,11 @@
 
     centre("wpo")
     w_copies["wpe"].wait()
-    wcat[...] = jnp.zeros_like(wcat)
-    wcat[0:4, 0:L] = wmf_ref[...].astype(F32)
-    wcat[:, L : 2 * L] = dot(wcat[:, 0:L].astype(BF16), weight("wpe"))
+    wmf[...] = jnp.zeros_like(wmf)
+    wmfp = jnp.concatenate([wmf_ref[...].astype(F32), jnp.zeros((12, L), F32)], axis=0).astype(BF16)
+    wmf[0:16, :] = wmfp
+    tpre[640:768, :] = jnp.zeros((128, L), BF16)
+    tpre[640:656, :] = dot(wmfp, weight("wpe")).astype(BF16)
 
     def landed(k):
         return pltpu.make_async_remote_copy(
@@ -289,12 +302,12 @@
         )
 
     def arrive(g, carry):
-        for i in range(2):
-            landed(2 * g + i).wait_recv()
-        mbuf[...] += encode(ein[pl.ds(2 * g, 2)], 2)
-        return carry
-
-    lax.fori_loop(0, 4, arrive, 0)
+        for i in range(4):
+            landed(4 * g + i).wait_recv()
+        mbuf[...] += encode(ein[pl.ds(4 * g, 4)], 4)
+        return carry
+
+    lax.fori_loop(0, 2, arrive, 0)
 
     w_copies["wni"].wait()
     w_copies["wno"].wait()
@@ -373,14 +386,15 @@
     w_copies["wpr"].wait()
     tpre[NODES : 2 * NODES, :] = dot(latent, weight("wpr")).astype(BF16)
 
+    def tall(b):
+        return pl.ds(pl.multiple_of(b * TALL, TALL), TALL)
+
     def ahead(b, carry):
-        rows = pl.ds(pl.multiple_of(b * BLK, BLK), BLK)
-        embed = dot_tn(featp[:, rows].astype(BF16), wcat[...].astype(BF16))
-        obuf[rows, :] = embed[:, 0:L].astype(BF16)
-        pre[rows, :] = dot(apre[rows, :], tpre[...]) + embed[:, L : 2 * L]
-        return carry
-
-    lax.fori_loop(0, AHEAD, ahead, 0)
+        obuf[tall(b), :] = dot(apre[tall(b), 640:768], wmf[...]).astype(BF16)
+        pre[tall(b), :] = dot(apre[tall(b), :], tpre[...])
+        return carry
+
+    ahead(0, 0)
 
     each(8, b1_copy, arrived)
     to_zx = hot(iota((256, 256), 1) == far_order(0))
@@ -393,17 +407,16 @@
     a2_in[zx] = a2_out[zx]
     b2_in[spot] = b2_out[spot]
 
-    lax.fori_loop(AHEAD, NBLK, ahead, 0)
+    ahead(1, 0)
 
     for e in range(8):
         near_copy(e).wait_recv()
 
     def near_part(b, carry):
-        rows = pl.ds(pl.multiple_of(b * BLK, BLK), BLK)
-        pre[rows, :] += dot(apost[rows, 0:512], tnear[...].reshape(512, L))
-        return carry
-
-    lax.fori_loop(0, NBLK, near_part, 0)
+        pre[tall(b), :] += dot(apost[tall(b), 0:512], tnear[...].reshape(512, L))
+        return carry
+
+    lax.fori_loop(0, MEDGES // TALL, near_part, 0)
 
     each(16, a2_copy, arrived)
     each(8, b2_copy, arrived)
@@ -488,6 +501,7 @@
             pltpu.VMEM((128, 128), I32),
             pltpu.VMEM((1, MEDGES), I32),
             pltpu.VMEM((CIN, GRID_N), BF16),
+            pltpu.VMEM((EDGES, GRID_N), BF16),
             pltpu.VMEM((EDGES, 256), BF16),
             pltpu.VMEM((CIN, L), BF16),
             pltpu.VMEM((256, L), F32),
@@ -495,17 +509,17 @@
             pltpu.VMEM((12, L, L), BF16),
             pltpu.VMEM((16, EDGES), F32),
             pltpu.VMEM((16, L), F32),
-            pltpu.VMEM((16, MEDGES), F32),
-            pltpu.VMEM((16, 2 * L), F32),
+            pltpu.VMEM((8, MEDGES), F32),
+            pltpu.VMEM((128, L), BF16),
             pltpu.VMEM((8, SLOT, 256), BF16),
             pltpu.VMEM((9, SLOT, 256), BF16),
             pltpu.VMEM((MEDGES // 128, 128, 128), I32),
             pltpu.VMEM((MEDGES // 128, 128, 128), I32),
-            pltpu.VMEM((MEDGES, 2 * NODES), BF16),
+            pltpu.VMEM((MEDGES, 768), BF16),
             pltpu.VMEM((MEDGES, 768), BF16),
             pltpu.VMEM((NODES, MEDGES), BF16),
             pltpu.VMEM((1024, NODES), BF16),
-            pltpu.VMEM((2 * NODES, L), BF16),
+            pltpu.VMEM((768, L), BF16),
             pltpu.VMEM((8, HCAP, L), BF16),
             pltpu.VMEM((256, L), BF16),
             pltpu.VMEM((8, HCAP, L), BF16),

time: 54.9 us -> 50.2 us (0.914)
  Pallas kernels: 48.9 us -> 44.2 us
    pallas_call x1, Pallas kernels: 48.9 us -> 44.2 us  [on_device(): pl.pallas_call(kernel, out_shape=(jax.ShapeDtypeStruct((NODES, L), BF16),...]
where the time goes in v4:
time: 50.2 us; the launch traced here: 49.9 us
  Pallas kernels  44.2 us (88%)
  local copies, waits for them, and re-layouts  5.12 us (10%)
  between operations  0.65 us (1%)
    pallas_call x1, Pallas kernels, on_device(): pl.pallas_call(kernel, out_shape=(jax.ShapeDtypeStruct((NODES, L), BF16),...  44.2 us
    unnamed x2, local copies, waits for them, and re-layouts  5.12 us

profile of v4, /device:TPU:1, one launch (start us, length us, event | category | flops | bytes accessed | tf_op | source)
XLA Modules:
  0.0 49.9 jit_solution(2980727746071261111)
XLA Ops:
  0.6 44.2 %shard_map.248 = (bf16[320,512]{1,0:T(8,128)(2,1)}, bf16[2560,512]{1,0:T(8,128)(2,1)}) custom-call(bf16[227,1024]{1,0:T(8,128)(2,1)} %bitcast.6, s32[768]{0:T(1024)} %send_ref.1, s32[1,768]{1,0:T(1,128)} %bitcast.8, s32[768]{0:T(1024)} %recv_ref.1, bf16[4,768]{1,0:T(4,128)(2,1)} %gfeat_ref.1, s32[8,64]{1,0:T(8,128)} %bitcast.7, s32[2,128]{1,0:T(2,128)} %bitcast.9, ...), custom_call_target="tpu_custom_call" | custom-call | flops 15000000512 | bytes 12000000 | tf_op jit(solution)/shard_map/pallas_call | solution.py:492
  44.8 1.7 %copy.29 = bf16[320,512]{1,0:T(8,128)(2,1)} copy(bf16[320,512]{1,0:T(8,128)(2,1)} %get-tuple-element.4) | data formatting | bytes 655360
  46.5 3.4 %copy.30 = bf16[2560,512]{1,0:T(8,128)(2,1)} copy(bf16[2560,512]{1,0:T(8,128)(2,1)} %get-tuple-element.5) | data formatting | bytes 5242880

commit v5 on v4

--- a/solution.py
+++ b/solution.py
@@ -23,6 +23,7 @@
 HCAP = 64
 SLOT = CAP + 16
 TALL = 1280
+PIECES = 8
 BLK = 640
 NBLK = MEDGES // BLK
 
@@ -90,8 +91,8 @@
     idx, mrow_ref, graw, pick, gsel, wraw, wpad32, wgi, wts, aux, wefp, featp, wmf,
     eout, ein, scol, rcol, apre, apost, rmask, gsend,
     tpre, tnear, tfar, near_out, a1_out, a1_in, b1_out, b1_in, b2_out, b2_in, a2_out, a2_in, hbuf,
-    pre, obuf, lat_buf, mbuf,
-    in_sem, w_sem, es_sem, er_sem, ns_sem, nr_sem, a1s, a1r, b1s, b1r, b2s, b2r, a2s, a2r, o_sem,
+    pre, lat_buf, mbuf,
+    in_sem, w_sem, es_sem, er_sem, ns_sem, nr_sem, a1s, a1r, b1s, b1r, b2s, b2r, a2s, a2r,
 ):
     lat = lax.axis_index("lat")
     lon = lax.axis_index("lon")
@@ -390,7 +391,7 @@
         return pl.ds(pl.multiple_of(b * TALL, TALL), TALL)
 
     def ahead(b, carry):
-        obuf[tall(b), :] = dot(apre[tall(b), 640:768], wmf[...]).astype(BF16)
+        edge_out[tall(b), :] = dot(apre[tall(b), 640:768], wmf[...]).astype(BF16)
         pre[tall(b), :] = dot(apre[tall(b), :], tpre[...])
         return carry
 
@@ -425,17 +426,13 @@
 
     mbuf[...] = jnp.zeros_like(mbuf)
 
-    def out_copy(b):
-        rows = pl.ds(pl.multiple_of(b * BLK, BLK), BLK)
-        return pltpu.make_async_copy(obuf.at[rows], edge_out.at[rows], o_sem.at[b])
-
     def hidden(b):
         rows = pl.ds(pl.multiple_of(b * BLK, BLK), BLK)
         return silu(pre[rows, :] + dot(apost[rows, 512:768], tfar[...])).astype(BF16)
 
     def finish(b, h):
         rows = pl.ds(pl.multiple_of(b * BLK, BLK), BLK)
-        return (obuf[rows, :].astype(F32) + scaled(dot(h, weight("wpo")))).astype(BF16)
+        return (edge_out[rows, :].astype(F32) + scaled(dot(h, weight("wpo")))).astype(BF16)
 
     hbuf[0] = hidden(0)
 
@@ -444,17 +441,15 @@
         out = finish(b, hbuf[lax.rem(b, 2)])
         ahead_h = hidden(b + 1)
         total = mbuf[...] + dot(rmask[:, rows], out)
-        obuf[rows, :] = out
+        edge_out[rows, :] = out
         hbuf[lax.rem(b + 1, 2)] = ahead_h
         mbuf[...] = total
-        out_copy(b).start()
         return carry
 
     lax.fori_loop(0, NBLK - 1, process, 0)
     last = NBLK - 1
     out = finish(last, hbuf[last % 2])
-    obuf[last * BLK : MEDGES, :] = out
-    out_copy(last).start()
+    edge_out[last * BLK : MEDGES, :] = out
     edge_sum = (mbuf[...] + dot(rmask[:, last * BLK : MEDGES], out)).astype(BF16)
 
     w_copies["wus"].wait()
@@ -473,11 +468,16 @@
     each(16, a2_copy, gone)
     each(8, b2_copy, gone)
 
-    def o_sent(b, carry):
-        out_copy(b).wait()
-        return carry
-
-    lax.fori_loop(0, NBLK, o_sent, 0)
+
+def hand_out(mesh_from, edge_from, mesh_to, edge_to, sems):
+    copies = [pltpu.make_async_copy(mesh_from, mesh_to, sems.at[0])]
+    for b in range(PIECES):
+        rows = pl.ds(b * (MEDGES // PIECES), MEDGES // PIECES)
+        copies.append(pltpu.make_async_copy(edge_from.at[rows], edge_to.at[rows], sems.at[1 + b]))
+    for copy in copies:
+        copy.start()
+    for copy in copies:
+        copy.wait()
 
 
 def on_device(
@@ -489,14 +489,14 @@
     vm = pl.BlockSpec(memory_space=pltpu.VMEM)
     hb = pl.BlockSpec(memory_space=pl.ANY)
     dma = pltpu.SemaphoreType.DMA
-    return pl.pallas_call(
+    mesh_rows, edge_rows = pl.pallas_call(
         kernel,
         out_shape=(
-            jax.ShapeDtypeStruct((NODES, L), BF16),
-            jax.ShapeDtypeStruct((MEDGES, L), BF16),
+            pltpu.VMEM((NODES, L), BF16),
+            pltpu.VMEM((MEDGES, L), BF16),
         ),
         in_specs=[hb, vm, vm, vm, vm, vm, vm, vm, vm, vm, hb, vm, vm] + [hb] * 12,
-        out_specs=(vm, hb),
+        out_specs=(vm, vm),
         scratch_shapes=[
             pltpu.VMEM((128, 128), I32),
             pltpu.VMEM((1, MEDGES), I32),
@@ -533,7 +533,6 @@
             pltpu.VMEM((16, 16, 256), BF16),
             pltpu.VMEM((2, BLK, L), BF16),
             pltpu.VMEM((MEDGES, L), F32),
-            pltpu.VMEM((MEDGES, L), BF16),
             pltpu.VMEM((NODES, L), BF16),
             pltpu.VMEM((NODES, L), F32),
             dma((2,)),
@@ -550,10 +549,9 @@
             dma((8,)),
             dma((16,)),
             dma((16,)),
-            dma((NBLK,)),
         ],
         compiler_params=pltpu.CompilerParams(
-            collective_id=0, has_side_effects=True, vmem_limit_bytes=60 * 1024 * 1024
+            collective_id=0, has_side_effects=True, vmem_limit_bytes=54 * 1024 * 1024
         ),
         cost_estimate=pl.CostEstimate(flops=15_000_000_000, bytes_accessed=12_000_000, transcendentals=4_000_000),
     )(
@@ -562,6 +560,17 @@
         w_grid_out, w_edge_latent, w_edge_out, w_node_in, w_node_out, w_proc_edge, w_proc_send, w_proc_recv,
         w_proc_out, w_upd_self, w_upd_sum, w_upd_out,
     )
+
+    return pl.pallas_call(
+        hand_out,
+        out_shape=(
+            jax.ShapeDtypeStruct((NODES, L), BF16),
+            jax.ShapeDtypeStruct((MEDGES, L), BF16),
+        ),
+        in_specs=[vm, vm],
+        out_specs=(hb, hb),
+        scratch_shapes=[dma((1 + PIECES,))],
+    )(mesh_rows, edge_rows)
 
 
 def solution(mesh):

time: 50.2 us -> 50 us (level)
  local copies, waits for them, and re-layouts: 5.12 us -> 2.23 us
  Pallas kernels: 44.2 us -> 46.9 us
    unnamed x2 -> x4, local copies, waits for them, and re-layouts: 5.12 us -> 2.23 us
    pallas_call x1 -> x2, Pallas kernels: 44.2 us -> 46.9 us  [the longest x1 43.4 us: on_device(): pl.pallas_call(kernel, out_shape=(pltpu.VMEM((NODES, L), BF16), pltpu.VME...]
where the time goes in v5:
time: 50 us; the launch traced here: 49.8 us
  Pallas kernels  46.9 us (94%)
  local copies, waits for them, and re-layouts  2.23 us (4%)
  between operations  0.66 us (1%)
    pallas_call x1, Pallas kernels, on_device(): pl.pallas_call(kernel, out_shape=(pltpu.VMEM((NODES, L), BF16), pltpu.VME...  43.4 us
    pallas_call x1, Pallas kernels, on_device(): pl.pallas_call(hand_out, out_shape=(jax.ShapeDtypeStruct((NODES, L), BF16...  3.52 us
    unnamed x4, local copies, waits for them, and re-layouts  2.23 us

profile of v5, /device:TPU:1, one launch (start us, length us, event | category | flops | bytes accessed | tf_op | source)
XLA Modules:
  0.0 49.8 jit_solution(11129896847342735121)
XLA Ops:
  0.6 43.4 %shard_map.248 = (bf16[320,512]{1,0:T(8,128)(2,1)S(1)}, bf16[2560,512]{1,0:T(8,128)(2,1)S(1)}) custom-call(bf16[227,1024]{1,0:T(8,128)(2,1)} %bitcast.6, s32[768]{0:T(1024)} %send_ref.1, s32[1,768]{1,0:T(1,128)} %bitcast.8, s32[768]{0:T(1024)} %recv_ref.1, bf16[4,768]{1,0:T(4,128)(2,1)} %gfeat_ref.1, s32[8,64]{1,0:T(8,128)} %bitcast.7, s32[2,128]{1,0:T(2,128)} %bitcast.9, ...), custom_call_target="tpu_custom_call" | custom-call | flops 15000000512 | bytes 12000000 | tf_op jit(solution)/shard_map/pallas_call | solution.py:492
  44.0 0.0 copy-start
  44.0 1.5 %copy-done = bf16[2560,512]{1,0:T(8,128)(2,1)} copy-done((bf16[2560,512]{1,0:T(8,128)(2,1)}, bf16[2560,512]{1,0:T(8,128)(2,1)S(1)}, u32[]{:S(2)}) %copy-start) | copy-done | bytes 2621464
  45.5 0.0 copy-start.1
  45.5 0.7 %copy-done.1 = bf16[320,512]{1,0:T(8,128)(2,1)} copy-done((bf16[320,512]{1,0:T(8,128)(2,1)}, bf16[320,512]{1,0:T(8,128)(2,1)S(1)}, u32[]{:S(2)}) %copy-start.1) | copy-done | bytes 327704
  46.3 3.5 %shard_map.249 = (bf16[320,512]{1,0:T(8,128)(2,1)}, bf16[2560,512]{1,0:T(8,128)(2,1)}) custom-call(bf16[320,512]{1,0:T(8,128)(2,1)} %copy-done.1, bf16[2560,512]{1,0:T(8,128)(2,1)} %copy-done), custom_call_target="tpu_custom_call" | custom-call | tf_op jit(solution)/shard_map/pallas_call | solution.py:564
Async XLA Ops:
  44.0 1.5 %copy-start = (bf16[2560,512]{1,0:T(8,128)(2,1)}, bf16[2560,512]{1,0:T(8,128)(2,1)S(1)}, u32[]{:S(2)}) copy-start(bf16[2560,512]{1,0:T(8,128)(2,1)S(1)} %get-tuple-element.5.edge_from) | copy-start | bytes 7864324
  45.5 0.7 %copy-start.1 = (bf16[320,512]{1,0:T(8,128)(2,1)}, bf16[320,512]{1,0:T(8,128)(2,1)S(1)}, u32[]{:S(2)}) copy-start(bf16[320,512]{1,0:T(8,128)(2,1)S(1)} %get-tuple-element.4.mesh_from) | copy-start | bytes 983044

commit v6 on v5

--- a/solution.py
+++ b/solution.py
@@ -23,7 +23,6 @@
 HCAP = 64
 SLOT = CAP + 16
 TALL = 1280
-PIECES = 8
 BLK = 640
 NBLK = MEDGES // BLK
 
@@ -37,7 +36,7 @@
 COL_MR = 32
 
 W_NAMES = (
-    "wgo", "wel", "weo", "wni", "wno", "wpe", "wps", "wpr", "wpo", "wus", "wua", "wuo",
+    "wgo", "wel", "weo", "wni", "wno", "wpe", "wps", "wpr", "wpo",
 )
 
 
@@ -86,12 +85,11 @@
 def kernel(
     grid_hbm, send_ref, dest_ref, recv_ref, gfeat_ref, near_ref, far_ref, msend_ref, mrecv_ref, mfeat_ref,
     wgi_hbm, wef_ref, wmf_ref,
-    wgo_h, wel_h, weo_h, wni_h, wno_h, wpe_h, wps_h, wpr_h, wpo_h, wus_h, wua_h, wuo_h,
-    mesh_out, edge_out,
+    wgo_h, wel_h, weo_h, wni_h, wno_h, wpe_h, wps_h, wpr_h, wpo_h,
+    pre, embed_out, far_mask, rmask, tfar, lat_buf, wpo_out,
     idx, mrow_ref, graw, pick, gsel, wraw, wpad32, wgi, wts, aux, wefp, featp, wmf,
-    eout, ein, scol, rcol, apre, apost, rmask, gsend,
-    tpre, tnear, tfar, near_out, a1_out, a1_in, b1_out, b1_in, b2_out, b2_in, a2_out, a2_in, hbuf,
-    pre, lat_buf, mbuf,
+    eout, ein, scol, rcol, apre, apost, gsend,
+    tpre, tnear, near_out, a1_out, a1_in, b1_out, b1_in, b2_out, b2_in, a2_out, a2_in, mbuf,
     in_sem, w_sem, es_sem, er_sem, ns_sem, nr_sem, a1s, a1r, b1s, b1r, b2s, b2r, a2s, a2r,
 ):
     lat = lax.axis_index("lat")
@@ -135,7 +133,7 @@
     wi_copy.start()
     w_copies = {}
     for k, (name, ref) in enumerate(
-        zip(W_NAMES, (wgo_h, wel_h, weo_h, wni_h, wno_h, wpe_h, wps_h, wpr_h, wpo_h, wus_h, wua_h, wuo_h))
+        zip(W_NAMES, (wgo_h, wel_h, weo_h, wni_h, wno_h, wpe_h, wps_h, wpr_h, wpo_h))
     ):
         w_copies[name] = pltpu.make_async_copy(ref, wts.at[k], w_sem.at[k])
         w_copies[name].start()
@@ -276,7 +274,7 @@
             apost[rows, t * 128 : (t + 1) * 128] = hot(s == lane + (NODES + t * 128))
         f = s - (NODES + 8 * HCAP)
         for t in range(2):
-            apost[rows, 512 + t * 128 : 512 + (t + 1) * 128] = hot(f == lane + t * 128)
+            far_mask[rows, t * 128 : (t + 1) * 128] = hot(f == lane + t * 128)
         lanes = pl.ds(pl.multiple_of(b * 128, 128), 128)
         apre[rows, 640:648] = jnp.transpose(featp[:, lanes]).astype(BF16)
         rmask[:, lanes] = hot(iota((NODES, 128), 0) == mrow_ref[:, lanes])
@@ -285,6 +283,7 @@
     lax.fori_loop(0, MEDGES // 128, masks, 0)
 
     centre("wpo")
+    wpo_out[...] = weight("wpo")
     w_copies["wpe"].wait()
     wmf[...] = jnp.zeros_like(wmf)
     wmfp = jnp.concatenate([wmf_ref[...].astype(F32), jnp.zeros((12, L), F32)], axis=0).astype(BF16)
@@ -391,7 +390,7 @@
         return pl.ds(pl.multiple_of(b * TALL, TALL), TALL)
 
     def ahead(b, carry):
-        edge_out[tall(b), :] = dot(apre[tall(b), 640:768], wmf[...]).astype(BF16)
+        embed_out[tall(b), :] = dot(apre[tall(b), 640:768], wmf[...]).astype(BF16)
         pre[tall(b), :] = dot(apre[tall(b), :], tpre[...])
         return carry
 
@@ -424,41 +423,6 @@
     tfar[:, 0:256] = dot(to_zx, b2_in[...].reshape(256, 256)).astype(BF16)
     tfar[:, 256:512] = a2_in[...].reshape(256, 256)
 
-    mbuf[...] = jnp.zeros_like(mbuf)
-
-    def hidden(b):
-        rows = pl.ds(pl.multiple_of(b * BLK, BLK), BLK)
-        return silu(pre[rows, :] + dot(apost[rows, 512:768], tfar[...])).astype(BF16)
-
-    def finish(b, h):
-        rows = pl.ds(pl.multiple_of(b * BLK, BLK), BLK)
-        return (edge_out[rows, :].astype(F32) + scaled(dot(h, weight("wpo")))).astype(BF16)
-
-    hbuf[0] = hidden(0)
-
-    def process(b, carry):
-        rows = pl.ds(pl.multiple_of(b * BLK, BLK), BLK)
-        out = finish(b, hbuf[lax.rem(b, 2)])
-        ahead_h = hidden(b + 1)
-        total = mbuf[...] + dot(rmask[:, rows], out)
-        edge_out[rows, :] = out
-        hbuf[lax.rem(b + 1, 2)] = ahead_h
-        mbuf[...] = total
-        return carry
-
-    lax.fori_loop(0, NBLK - 1, process, 0)
-    last = NBLK - 1
-    out = finish(last, hbuf[last % 2])
-    edge_out[last * BLK : MEDGES, :] = out
-    edge_sum = (mbuf[...] + dot(rmask[:, last * BLK : MEDGES], out)).astype(BF16)
-
-    w_copies["wus"].wait()
-    w_copies["wua"].wait()
-    w_copies["wuo"].wait()
-    h = dot(lat_buf[...], weight("wus")) + dot(edge_sum, weight("wua"))
-    h = silu(h).astype(BF16)
-    mesh_out[...] = (lat_buf[...].astype(F32) + normalize(dot(h, weight("wuo")))).astype(BF16)
-
     for k in range(8):
         edge_copy(k).wait_send()
         near_copy(k).wait_send()
@@ -469,15 +433,44 @@
     each(8, b2_copy, gone)
 
 
-def hand_out(mesh_from, edge_from, mesh_to, edge_to, sems):
-    copies = [pltpu.make_async_copy(mesh_from, mesh_to, sems.at[0])]
-    for b in range(PIECES):
-        rows = pl.ds(b * (MEDGES // PIECES), MEDGES // PIECES)
-        copies.append(pltpu.make_async_copy(edge_from.at[rows], edge_to.at[rows], sems.at[1 + b]))
-    for copy in copies:
+def finish_kernel(
+    pre, embed, far_mask, rmask, tfar, lat_buf, wpo, wus_h, wua_h, wuo_h, mesh_out, edge_out,
+    wts, obuf, hbuf, mbuf, w_sem, o_sem,
+):
+    w_copies = [pltpu.make_async_copy(ref, wts.at[k], w_sem.at[k]) for k, ref in enumerate((wus_h, wua_h, wuo_h))]
+    for copy in w_copies:
         copy.start()
-    for copy in copies:
+
+    def out_copy(b):
+        rows = pl.ds(b * BLK, BLK)
+        return pltpu.make_async_copy(obuf.at[rows], edge_out.at[rows], o_sem.at[b])
+
+    def hidden(b):
+        rows = pl.ds(b * BLK, BLK)
+        return silu(pre[rows, :] + dot(far_mask[rows, :], tfar[...])).astype(BF16)
+
+    def finish(b, h):
+        rows = pl.ds(b * BLK, BLK)
+        return (embed[rows, :].astype(F32) + scaled(dot(h, wpo[...]))).astype(BF16)
+
+    mbuf[...] = jnp.zeros_like(mbuf)
+    hbuf[0] = hidden(0)
+    for b in range(NBLK):
+        rows = pl.ds(b * BLK, BLK)
+        out = finish(b, hbuf[b % 2])
+        if b + 1 < NBLK:
+            hbuf[(b + 1) % 2] = hidden(b + 1)
+        obuf[rows, :] = out
+        out_copy(b).start()
+        mbuf[...] += dot(rmask[:, rows], out)
+
+    for copy in w_copies:
         copy.wait()
+    h = dot(lat_buf[...], wts[0]) + dot(mbuf[...].astype(BF16), wts[1])
+    h = silu(h).astype(BF16)
+    mesh_out[...] = (lat_buf[...].astype(F32) + normalize(dot(h, wts[2]))).astype(BF16)
+    for b in range(NBLK):
+        out_copy(b).wait()
 
 
 def on_device(
@@ -489,14 +482,19 @@
     vm = pl.BlockSpec(memory_space=pltpu.VMEM)
     hb = pl.BlockSpec(memory_space=pl.ANY)
     dma = pltpu.SemaphoreType.DMA
-    mesh_rows, edge_rows = pl.pallas_call(
+    kept = pl.pallas_call(
         kernel,
         out_shape=(
+            pltpu.VMEM((MEDGES, L), F32),
+            pltpu.VMEM((MEDGES, L), BF16),
+            pltpu.VMEM((MEDGES, 256), BF16),
+            pltpu.VMEM((NODES, MEDGES), BF16),
+            pltpu.VMEM((256, L), BF16),
             pltpu.VMEM((NODES, L), BF16),
-            pltpu.VMEM((MEDGES, L), BF16),
+            pltpu.VMEM((L, L), BF16),
         ),
-        in_specs=[hb, vm, vm, vm, vm, vm, vm, vm, vm, vm, hb, vm, vm] + [hb] * 12,
-        out_specs=(vm, vm),
+        in_specs=[hb, vm, vm, vm, vm, vm, vm, vm, vm, vm, hb, vm, vm] + [hb] * 9,
+        out_specs=(vm,) * 7,
         scratch_shapes=[
             pltpu.VMEM((128, 128), I32),
             pltpu.VMEM((1, MEDGES), I32),
@@ -506,7 +504,7 @@
             pltpu.VMEM((CIN, L), BF16),
             pltpu.VMEM((256, L), F32),
             pltpu.VMEM((256, L), BF16),
-            pltpu.VMEM((12, L, L), BF16),
+            pltpu.VMEM((9, L, L), BF16),
             pltpu.VMEM((16, EDGES), F32),
             pltpu.VMEM((16, L), F32),
             pltpu.VMEM((8, MEDGES), F32),
@@ -516,12 +514,10 @@
             pltpu.VMEM((MEDGES // 128, 128, 128), I32),
             pltpu.VMEM((MEDGES // 128, 128, 128), I32),
             pltpu.VMEM((MEDGES, 768), BF16),
-            pltpu.VMEM((MEDGES, 768), BF16),
-            pltpu.VMEM((NODES, MEDGES), BF16),
+            pltpu.VMEM((MEDGES, 512), BF16),
             pltpu.VMEM((1024, NODES), BF16),
             pltpu.VMEM((768, L), BF16),
             pltpu.VMEM((8, HCAP, L), BF16),
-            pltpu.VMEM((256, L), BF16),
             pltpu.VMEM((8, HCAP, L), BF16),
             pltpu.VMEM((16, 16, 256), BF16),
             pltpu.VMEM((16, 16, 256), BF16),
@@ -531,12 +527,9 @@
             pltpu.VMEM((8, 32, 256), BF16),
             pltpu.VMEM((16, 16, 256), BF16),
             pltpu.VMEM((16, 16, 256), BF16),
-            pltpu.VMEM((2, BLK, L), BF16),
-            pltpu.VMEM((MEDGES, L), F32),
-            pltpu.VMEM((NODES, L), BF16),
             pltpu.VMEM((NODES, L), F32),
             dma((2,)),
-            dma((12,)),
+            dma((9,)),
             dma((8,)),
             dma((8,)),
             dma((8,)),
@@ -551,26 +544,35 @@
             dma((16,)),
         ],
         compiler_params=pltpu.CompilerParams(
-            collective_id=0, has_side_effects=True, vmem_limit_bytes=54 * 1024 * 1024
+            collective_id=0, has_side_effects=True, vmem_limit_bytes=44 * 1024 * 1024
         ),
         cost_estimate=pl.CostEstimate(flops=15_000_000_000, bytes_accessed=12_000_000, transcendentals=4_000_000),
     )(
         grid_in.T, g2m_senders, g2m_dest.reshape(1, EDGES), g2m_receivers, g2m_feat,
         halo_near.reshape(8, HCAP), halo_far.reshape(128, 2).T, mesh_senders, mesh_receivers, mesh_feat, w_grid_in, w_edge_feat, w_mesh_feat,
         w_grid_out, w_edge_latent, w_edge_out, w_node_in, w_node_out, w_proc_edge, w_proc_send, w_proc_recv,
-        w_proc_out, w_upd_self, w_upd_sum, w_upd_out,
+        w_proc_out,
     )
 
     return pl.pallas_call(
-        hand_out,
+        finish_kernel,
         out_shape=(
             jax.ShapeDtypeStruct((NODES, L), BF16),
             jax.ShapeDtypeStruct((MEDGES, L), BF16),
         ),
-        in_specs=[vm, vm],
-        out_specs=(hb, hb),
-        scratch_shapes=[dma((1 + PIECES,))],
-    )(mesh_rows, edge_rows)
+        in_specs=[vm] * 7 + [hb] * 3,
+        out_specs=(vm, hb),
+        scratch_shapes=[
+            pltpu.VMEM((3, L, L), BF16),
+            pltpu.VMEM((MEDGES, L), BF16),
+            pltpu.VMEM((2, BLK, L), BF16),
+            pltpu.VMEM((NODES, L), F32),
+            dma((3,)),
+            dma((NBLK,)),
+        ],
+        compiler_params=pltpu.CompilerParams(vmem_limit_bytes=20 * 1024 * 1024),
+        cost_estimate=pl.CostEstimate(flops=4_000_000_000, bytes_accessed=5_000_000, transcendentals=1_500_000),
+    )(*kept, w_upd_self, w_upd_sum, w_upd_out)
 
 
 def solution(mesh):

time: 50 us -> 44.3 us (0.89)
  Pallas kernels: 46.9 us -> 43.3 us
  local copies, waits for them, and re-layouts: 2.23 us -> 0.01 us
    pallas_call x2, Pallas kernels: 46.9 us -> 43.3 us  [the longest x1 37.1 us: on_device(): pl.pallas_call(kernel, out_shape=(pltpu.VMEM((MEDGES, L), F32), pltpu.VME...]
    unnamed x4 -> x6, local copies, waits for them, and re-layouts: 2.23 us -> 0.01 us
where the time goes in v6:
time: 44.3 us; the launch traced here: 44.2 us
  Pallas kernels  43.3 us (98%)
  between operations  0.86 us (2%)
    pallas_call x1, Pallas kernels, on_device(): pl.pallas_call(kernel, out_shape=(pltpu.VMEM((MEDGES, L), F32), pltpu.VME...  37.1 us
    pallas_call x1, Pallas kernels, on_device(): pl.pallas_call(finish_kernel, out_shape=(jax.ShapeDtypeStruct((NODES, L),...  6.2 us

profile of v6, /device:TPU:1, one launch (start us, length us, event | category | flops | bytes accessed | tf_op | source)
XLA Modules:
  0.0 44.2 jit_solution(8746648838440719959)
XLA Ops:
  0.6 0.0 copy-start
  0.6 0.0 copy-start.1
  0.7 0.0 copy-start.2
  0.7 37.1 %shard_map.248 = (f32[2560,512]{1,0:T(8,128)S(1)}, bf16[2560,512]{1,0:T(8,128)(2,1)S(1)}, bf16[2560,256]{1,0:T(8,128)(2,1)S(1)}, bf16[320,2560]{1,0:T(8,128)(2,1...) custom-call(bf16[227,1024]{1,0:T(8,128)(2,1)} %bitcast.6, ...), custom_call_target="tpu_custom_call" | custom-call | flops 15000000512 | bytes 12000000 | tf_op jit(solution)/shard_map/pallas_call | solution.py:485
  37.8 0.0 copy-done
  37.8 0.0 copy-done.1
  37.8 0.0 copy-done.2
  37.8 6.2 %shard_map.249 = (bf16[320,512]{1,0:T(8,128)(2,1)}, bf16[2560,512]{1,0:T(8,128)(2,1)}) custom-call(f32[2560,512]{1,0:T(8,128)S(1)} %get-tuple-element.9.pre, bf16[2560,512]{1,0:T(8,128)(2,1)S(1)} %get-tuple-element.10.embed, bf16[2560,256]{1,0:T(8,128)(2,1)S(1)} %get-tuple-element.11.far_mask, bf16[320,2560]{1,0:T(8,128)(2,1)S(1)} %get-tuple-element.12.rmask, ...), custom_call_target="tpu_custom_call" | custom-call | flops 4000000000 | bytes 5000000 | tf_op jit(solution)/shard_map/pallas_call | solution.py:557
Async XLA Ops:
  0.6 37.1 %copy-start = (bf16[512,512]{1,0:T(8,128)(2,1)S(1)}, bf16[512,512]{1,0:T(8,128)(2,1)}, u32[]{:S(2)}) copy-start(bf16[512,512]{1,0:T(8,128)(2,1)} %wus_h.1) | copy-start | bytes 1572868
  0.6 37.1 %copy-start.1 = (bf16[512,512]{1,0:T(8,128)(2,1)S(1)}, bf16[512,512]{1,0:T(8,128)(2,1)}, u32[]{:S(2)}) copy-start(bf16[512,512]{1,0:T(8,128)(2,1)} %wua_h.1) | copy-start | bytes 1572868
  0.7 37.1 %copy-start.2 = (bf16[512,512]{1,0:T(8,128)(2,1)S(1)}, bf16[512,512]{1,0:T(8,128)(2,1)}, u32[]{:S(2)}) copy-start(bf16[512,512]{1,0:T(8,128)(2,1)} %wuo_h.1) | copy-start | bytes 1572868

commit v7 on v6

--- a/solution.py
+++ b/solution.py
@@ -23,7 +23,7 @@
 HCAP = 64
 SLOT = CAP + 16
 TALL = 1280
-BLK = 640
+BLK = 1280
 NBLK = MEDGES // BLK
 
 CODES = (1, 7, 3, 5, 0, 2, 6, 8)
@@ -378,8 +378,6 @@
         )
 
     near_out[...] = dot(gsend[0:512, :], own).astype(BF16).reshape(8, HCAP, L)
-    for e in (0, 2, 5, 7, 3, 4, 1, 6):
-        near_copy(e).start()
     a1_in[zx] = a1_out[zx]
     b1_in[spot] = b1_out[spot]
 
@@ -395,6 +393,8 @@
         return carry
 
     ahead(0, 0)
+    for e in (0, 2, 5, 7, 3, 4, 1, 6):
+        near_copy(e).start()
 
     each(8, b1_copy, arrived)
     to_zx = hot(iota((256, 256), 1) == far_order(0))

time: 44.3 us -> 43.2 us (0.975); the launches traced: 44.2 us -> 42.5 us
  Pallas kernels: 43.3 us -> 41.7 us
    pallas_call x1, Pallas kernels: 37.1 us -> 36 us  [on_device(): pl.pallas_call(kernel, out_shape=(pltpu.VMEM((MEDGES, L), F32), pltpu.VME...]
    pallas_call x1, Pallas kernels: 6.2 us -> 5.63 us  [on_device(): pl.pallas_call(finish_kernel, out_shape=(jax.ShapeDtypeStruct((NODES, L),...]
where the time goes in v7:
time: 43.2 us; the launch traced here: 42.5 us
  Pallas kernels  41.7 us (97%)
  between operations  0.86 us (2%)
    pallas_call x1, Pallas kernels, on_device(): pl.pallas_call(kernel, out_shape=(pltpu.VMEM((MEDGES, L), F32), pltpu.VME...  36 us
    pallas_call x1, Pallas kernels, on_device(): pl.pallas_call(finish_kernel, out_shape=(jax.ShapeDtypeStruct((NODES, L),...  5.63 us

profile of v7, /device:TPU:1, one launch (start us, length us, event | category | flops | bytes accessed | tf_op | source)
XLA Modules:
  0.0 42.5 jit_solution(14379399934733234284)
XLA Ops:
  0.6 0.0 copy-start
  0.6 0.0 copy-start.1
  0.7 0.0 copy-start.2
  0.7 36.0 %shard_map.248 = (f32[2560,512]{1,0:T(8,128)S(1)}, bf16[2560,512]{1,0:T(8,128)(2,1)S(1)}, bf16[2560,256]{1,0:T(8,128)(2,1)S(1)}, bf16[320,2560]{1,0:T(8,128)(2,1...) custom-call(bf16[227,1024]{1,0:T(8,128)(2,1)} %bitcast.6, ...), custom_call_target="tpu_custom_call" | custom-call | flops 15000000512 | bytes 12000000 | tf_op jit(solution)/shard_map/pallas_call | solution.py:485
  36.7 0.0 copy-done
  36.7 0.0 copy-done.1
  36.7 0.0 copy-done.2
  36.8 5.6 %shard_map.249 = (bf16[320,512]{1,0:T(8,128)(2,1)}, bf16[2560,512]{1,0:T(8,128)(2,1)}) custom-call(f32[2560,512]{1,0:T(8,128)S(1)} %get-tuple-element.9.pre, bf16[2560,512]{1,0:T(8,128)(2,1)S(1)} %get-tuple-element.10.embed, bf16[2560,256]{1,0:T(8,128)(2,1)S(1)} %get-tuple-element.11.far_mask, bf16[320,2560]{1,0:T(8,128)(2,1)S(1)} %get-tuple-element.12.rmask, ...), custom_call_target="tpu_custom_call" | custom-call | flops 4000000000 | bytes 5000000 | tf_op jit(solution)/shard_map/pallas_call | solution.py:557
Async XLA Ops:
  0.6 36.1 %copy-start = (bf16[512,512]{1,0:T(8,128)(2,1)S(1)}, bf16[512,512]{1,0:T(8,128)(2,1)}, u32[]{:S(2)}) copy-start(bf16[512,512]{1,0:T(8,128)(2,1)} %wus_h.1) | copy-start | bytes 1572868
  0.6 36.1 %copy-start.1 = (bf16[512,512]{1,0:T(8,128)(2,1)S(1)}, bf16[512,512]{1,0:T(8,128)(2,1)}, u32[]{:S(2)}) copy-start(bf16[512,512]{1,0:T(8,128)(2,1)} %wua_h.1) | copy-start | bytes 1572868
  0.7 36.1 %copy-start.2 = (bf16[512,512]{1,0:T(8,128)(2,1)S(1)}, bf16[512,512]{1,0:T(8,128)(2,1)}, u32[]{:S(2)}) copy-start(bf16[512,512]{1,0:T(8,128)(2,1)} %wuo_h.1) | copy-start | bytes 1572868
